TPU v7x, 512 devices: a whole 4x8x8 slice. The times are simulated.
512 devices in a mesh: horiz: 64 (over x, z, core), lev: 8 (over y).
Axes of the slice: x: 4, y: 8, z: 8, core: 2. Of those that a mesh axis runs over, the one named last changes fastest.
Arguments:
- prior_state: float32 [80, 8, 262144], P(None, 'lev', 'horiz'), may hold values from -6 to 6
- localization: float32 [6, 128, 8, 2048], P(None, None, 'lev', 'horiz'), may hold values from 0.1 to 1
- observed: float32 [6, 128], replicated, may hold values from -5 to 5
- error_variance: float32 [6, 128], replicated, may hold values from 0.3 to 2
- owner_ids: int32 [6], replicated, may hold values from 0 to 63
- obs_cell: int32 [6, 128], replicated, may hold values from 0 to 4095
Outputs:
- posterior_state: float32 [80, 8, 262144], P(None, 'lev', 'horiz')
- obs_increments: float32 [6, 128, 80], replicated
All inputs are finite; a program needn't handle non-finite values.
Results may differ from a plain program's by a relative error of at most 0.0001.
Values sent between devices are 32-bit elements; how exact they have to be, the bound alone decides.
A program may use at most 64 MiB of HBM per device.

v0:
```python
import jax
import jax.numpy as jnp
from jax import lax
from jax.sharding import PartitionSpec as P

TILE = 128


highest = lax.Precision.HIGHEST


def spread(block, axis, holder):
    block = jnp.where(lax.axis_index(axis) == holder, block, jnp.zeros_like(block))
    return lax.psum(block, axis)


def batch_increment(priors, observed_now, variance):
    members = priors.shape[1]
    average = jnp.mean(priors, axis=1)
    deviation = priors - average[:, None]
    covariance = jnp.dot(deviation, deviation.T, precision=highest) / (members - 1)
    factor = jnp.linalg.cholesky(covariance + jnp.diag(variance))
    innovation = observed_now - average
    half_solved = jax.scipy.linalg.solve_triangular(factor, innovation, lower=True)
    gain_vector = jax.scipy.linalg.solve_triangular(factor, half_solved, lower=True, trans=1)
    mean_shift = jnp.dot(covariance, gain_vector, precision=highest)
    rooted = factor + jnp.diag(jnp.sqrt(variance))
    whitened = jax.scipy.linalg.solve_triangular(rooted, deviation, lower=True)
    unwhitened = jax.scipy.linalg.solve_triangular(factor, whitened, lower=True, trans=1)
    increment = mean_shift[:, None] - jnp.dot(covariance, unwhitened, precision=highest)
    half_gain = jax.scipy.linalg.solve_triangular(factor, increment, lower=True)
    gain_weights = jax.scipy.linalg.solve_triangular(factor, half_gain, lower=True, trans=1)
    return (increment, gain_weights)


def local(prior_state, localization, observed, error_variance, owner_ids, obs_cell):
    members, levels_here, cells_here = prior_state.shape
    batches, observations = obs_cell.shape
    rows_here = observations // lax.axis_size("lev")
    per_level = rows_here // levels_here
    tiles_here = cells_here // TILE
    ensemble = prior_state.reshape(members, levels_here * cells_here)
    level_local = jnp.arange(rows_here, dtype=jnp.int32) // per_level
    level_rank = lax.axis_index("lev")
    column_rank = lax.axis_index("horiz")
    divisor = members - 1.0

    def positions(batch_index):
        cell_index = lax.dynamic_slice_in_dim(
            obs_cell[batch_index], level_rank * rows_here, rows_here, 0
        )
        return (
            level_local * cells_here + cell_index,
            level_local * tiles_here + cell_index // TILE,
        )

    def regress(current, deviation, gain_weights, batch_index):
        covariance = jnp.dot(deviation, current, precision=highest)
        scaled = (
            covariance.reshape(observations, levels_here, tiles_here, TILE)
            * (localization[batch_index] / divisor)[..., None]
        )
        return current + jnp.dot(
            gain_weights.T,
            scaled.reshape(observations, levels_here * cells_here),
            precision=highest,
        )

    owned_rows = jnp.take(ensemble, positions(0)[0], axis=1).T
    collected = []
    for batch_index in range(batches):
        owner_rank = owner_ids[batch_index]
        observed_now = observed[batch_index]
        variance = error_variance[batch_index]
        column_rows = lax.all_gather(owned_rows, "lev", axis=0, tiled=True)
        local_increment, local_gain = lax.cond(
            column_rank == owner_rank,
            lambda rows_in: batch_increment(rows_in, observed_now, variance),
            lambda rows_in: (jnp.zeros_like(rows_in), jnp.zeros_like(rows_in)),
            column_rows,
        )
        priors, increment, gain_weights = (
            spread(column_rows, "horiz", owner_rank),
            spread(local_increment, "horiz", owner_rank),
            spread(local_gain, "horiz", owner_rank),
        )
        deviation = priors - jnp.mean(priors, axis=1)[:, None]
        collected.append(increment)
        if batch_index + 1 < batches:
            cell_pos, tile_pos = positions(batch_index + 1)
            ensemble = regress(ensemble, deviation, gain_weights, batch_index)
            owned_rows = jnp.take(ensemble, cell_pos, axis=1).T
        else:
            ensemble = regress(ensemble, deviation, gain_weights, batch_index)
    return (ensemble.reshape(members, levels_here, cells_here), jnp.stack(collected))


def solution(mesh):
    in_specs = (P(None, "lev", "horiz"), P(None, None, "lev", "horiz"), P(), P(), P(), P())
    out_specs = (P(None, "lev", "horiz"), P())
    return jax.shard_map(local, mesh=mesh, in_specs=in_specs, out_specs=out_specs, check_vma=False)
```

profile of v0, /device:TPU:1, one launch (start us, length us, event | category | flops | bytes accessed | tf_op | source)
XLA Modules:
  0.0 1508.5 jit_solution(9987054214759824077)
XLA Ops:
  8.2 4.0 copy.116
  12.2 2.3 gather_fusion
  14.6 20.6 %all_gather.18 = f32[128,80]{1,0:T(8,128)S(1)} all-gather(f32[16,80]{1,0:T(8,128)S(1)} %broadcast_select_fusion.17), channel_id=1, replica_groups=mesh['horiz'=64,'lev'=8] {'lev'}, dimensions={0}, use_global_device_ids=true | all-gather | bytes 46080 | tf_op jit(solution)/shard_map/all_gather | solution.py:75
  48.4 214.2 %all-reduce.23.cloned.1.call-done = (f32[128,80]{0,1:T(8,128)}, f32[128,80]{0,1:T(8,128)}) async-done(((f32[128,80]{0,1:T(8,128)}, f32[128,80]{0,1:T(8,128)}), (f32[128,80]{0,1:T(8,128)}, f32[128,80]{0,1:T(8,128)})) %all-reduce.23.cloned.1.call-update) | async-done | bytes 81936 | tf_op jit(solution)/shard_map/psum | solution.py:14
  263.4 4.6 convolution_multiply_fusion.11
  268.0 2.9 convolution_add_fusion.5
  273.1 19.5 %all_gather.19 = f32[128,80]{1,0:T(8,128)S(1)} all-gather(f32[16,80]{1,0:T(8,128)S(1)} %broadcast_select_fusion.16), channel_id=1, replica_groups=mesh['horiz'=64,'lev'=8] {'lev'}, dimensions={0}, use_global_device_ids=true | all-gather | bytes 46080 | tf_op jit(solution)/shard_map/all_gather | solution.py:75
  295.0 8.9 all-reduce.19.cloned.1.call-start
  304.5 202.2 %all-reduce.21.cloned.1.call-done = (f32[128,80]{0,1:T(8,128)}, f32[128,80]{0,1:T(8,128)}) async-done(((f32[128,80]{0,1:T(8,128)}, f32[128,80]{0,1:T(8,128)}), (f32[128,80]{0,1:T(8,128)}, f32[128,80]{0,1:T(8,128)})) %all-reduce.21.cloned.1.call-update) | async-done | bytes 81936 | tf_op jit(solution)/shard_map/psum | solution.py:14
  508.3 2.9 convolution_multiply_fusion.10
  511.2 1.3 convolution_add_fusion.4
  512.5 1.8 copy.102
  514.4 2.3 gather_fusion.2
  516.8 19.5 %all_gather.20 = f32[128,80]{1,0:T(8,128)S(1)} all-gather(f32[16,80]{1,0:T(8,128)S(1)} %broadcast_select_fusion.15), channel_id=1, replica_groups=mesh['horiz'=64,'lev'=8] {'lev'}, dimensions={0}, use_global_device_ids=true | all-gather | bytes 46080 | tf_op jit(solution)/shard_map/all_gather | solution.py:75
  539.3 215.5 %all-reduce.19.cloned.1.call-done = (f32[128,80]{0,1:T(8,128)}, f32[128,80]{0,1:T(8,128)}) async-done(((f32[128,80]{0,1:T(8,128)}, f32[128,80]{0,1:T(8,128)}), (f32[128,80]{0,1:T(8,128)}, f32[128,80]{0,1:T(8,128)})) %all-reduce.19.cloned.1.call-update) | async-done | bytes 81936 | tf_op jit(solution)/shard_map/psum | solution.py:14
  756.3 2.9 convolution_multiply_fusion.9
  759.2 1.3 convolution_add_fusion.3
  762.7 19.5 %all_gather.21 = f32[128,80]{1,0:T(8,128)S(1)} all-gather(f32[16,80]{1,0:T(8,128)S(1)} %broadcast_select_fusion.14), channel_id=1, replica_groups=mesh['horiz'=64,'lev'=8] {'lev'}, dimensions={0}, use_global_device_ids=true | all-gather | bytes 46080 | tf_op jit(solution)/shard_map/all_gather | solution.py:75
  785.1 210.8 %all-reduce.17.cloned.1.call-done = (f32[128,80]{0,1:T(8,128)}, f32[128,80]{0,1:T(8,128)}) async-done(((f32[128,80]{0,1:T(8,128)}, f32[128,80]{0,1:T(8,128)}), (f32[128,80]{0,1:T(8,128)}, f32[128,80]{0,1:T(8,128)})) %all-reduce.17.cloned.1.call-update) | async-done | bytes 81936 | tf_op jit(solution)/shard_map/psum | solution.py:14
  997.4 2.9 convolution_multiply_fusion.8
  1000.4 1.3 convolution_add_fusion.2
  1001.7 1.8 copy.108
  1003.6 2.3 gather_fusion.4
  1005.9 19.5 %all_gather.22 = f32[128,80]{1,0:T(8,128)S(1)} all-gather(f32[16,80]{1,0:T(8,128)S(1)} %broadcast_select_fusion.13), channel_id=1, replica_groups=mesh['horiz'=64,'lev'=8] {'lev'}, dimensions={0}, use_global_device_ids=true | all-gather | bytes 46080 | tf_op jit(solution)/shard_map/all_gather | solution.py:75
  1028.3 211.4 %all-reduce.15.cloned.1.call-done = (f32[128,80]{0,1:T(8,128)}, f32[128,80]{0,1:T(8,128)}) async-done(((f32[128,80]{0,1:T(8,128)}, f32[128,80]{0,1:T(8,128)}), (f32[128,80]{0,1:T(8,128)}, f32[128,80]{0,1:T(8,128)})) %all-reduce.15.cloned.1.call-update) | async-done | bytes 81936 | tf_op jit(solution)/shard_map/psum | solution.py:14
  1241.3 2.9 convolution_multiply_fusion.7
  1244.2 1.3 convolution_add_fusion.1
  1247.0 19.5 %all_gather.23 = f32[128,80]{1,0:T(8,128)S(1)} all-gather(f32[16,80]{1,0:T(8,128)S(1)} %broadcast_select_fusion.12), channel_id=1, replica_groups=mesh['horiz'=64,'lev'=8] {'lev'}, dimensions={0}, use_global_device_ids=true | all-gather | bytes 46080 | tf_op jit(solution)/shard_map/all_gather | solution.py:75
  1269.5 221.9 %all-reduce.13.cloned.1.call-done = (f32[128,80]{0,1:T(8,128)}, f32[128,80]{0,1:T(8,128)}, f32[1,128,80]{1,2,0:T(8,128)}, f32[1,128,80]{1,2,0:T(8,128)}, f32[1,1...) async-done(((f32[128,80]{0,1:T(8,128)}, f32[128,80]{0,1:T(8,128)}, f32[1,128,80]{1,2,0:T(8,128)}, ...) | async-done | bytes 327696 | tf_op jit(solution)/shard_map/psum | solution.py:14
  1493.6 2.9 convolution_multiply_fusion.6
  1496.6 1.4 fusion.138
  1498.0 2.4 copy.114
  (159 shorter events, 44.5 us)
Async XLA Ops:
  7.2 28.0 %copy-start.22 = (s32[6]{0:T(128)S(1)}, s32[6]{0:T(128)}, u32[]{:S(2)}) copy-start(s32[6]{0:T(128)} %param.33) | copy-start | bytes 76
  7.2 29.4 %copy-start.8 = (f32[6,128]{1,0:T(8,128)S(1)}, f32[6,128]{1,0:T(8,128)}, u32[]{:S(2)}) copy-start(f32[6,128]{1,0:T(8,128)} %param.31) | copy-start | bytes 9220
  7.2 255.4 %all-reduce.23.cloned.1.call-start = ((), (), s32[]{:S(2)}) async-start(), calls=%async_computation.5 | async-start | bytes 163840 | tf_op jit(solution)/shard_map/psum | solution.py:14
  12.2 25.9 %copy-start.9 = (f32[6,128,1,32]{1,3,2,0:T(8,128)S(1)}, f32[6,128,1,32]{1,3,2,0:T(8,128)}, u32[]{:S(2)}) copy-start(f32[6,128,1,32]{1,3,2,0:T(8,128)} %param.30) | copy-start | bytes 294916
  12.2 251.2 %copy-start = (f32[80,1,4096]{2,1,0:T(1,128)S(1)}, f32[80,1,4096]{2,1,0:T(1,128)}, u32[]{:S(2)}) copy-start(f32[80,1,4096]{2,1,0:T(1,128)} %param.29) | copy-start | bytes 3932164
  37.9 468.9 %all-reduce.21.cloned.1.call-start = ((), (), s32[]{:S(2)}) async-start(), calls=%async_computation.4 | async-start | bytes 163840 | tf_op jit(solution)/shard_map/psum | solution.py:14
  262.6 5.4 copy-start.11
  272.4 235.2 %copy-start.2 = (f32[128,32]{1,0:T(8,128)S(1)}, f32[128,32]{1,0:T(8,128)}, u32[]{:S(2)}) copy-start(f32[128,32]{1,0:T(8,128)} %copy.101) | copy-start | bytes 49156
  295.0 459.8 %all-reduce.19.cloned.1.call-start = ((), (), s32[]{:S(2)}) async-start(), calls=%async_computation.3 | async-start | bytes 163840 | tf_op jit(solution)/shard_map/psum | solution.py:14
  506.7 1.5 copy-start.4
  508.2 2.9 copy-start.13
  512.5 4.2 copy-start.26
  514.4 241.3 %copy-start.1 = (f32[128,32]{1,0:T(8,128)S(1)}, f32[128,32]{1,0:T(8,128)}, u32[]{:S(2)}) copy-start(f32[128,32]{1,0:T(8,128)} %copy.104) | copy-start | bytes 49156
  538.3 457.7 %all-reduce.17.cloned.1.call-start = ((), (), s32[]{:S(2)}) async-start(), calls=%async_computation.2 | async-start | bytes 163840 | tf_op jit(solution)/shard_map/psum | solution.py:14
  754.8 1.5 copy-start.5
  756.3 2.9 copy-start.14
  784.3 455.5 %all-reduce.15.cloned.1.call-start = ((), (), s32[]{:S(2)}) async-start(), calls=%async_computation.1 | async-start | bytes 163840 | tf_op jit(solution)/shard_map/psum | solution.py:14
  995.9 1.5 copy-start.6
  997.4 2.9 copy-start.15
  1001.7 4.1 copy-start.25
  1027.4 464.0 %all-reduce.13.cloned.1.call-start = ((), (), s32[]{:S(2)}) async-start(), calls=%async_computation | async-start | bytes 655360 | tf_op jit(solution)/shard_map/psum | solution.py:14
  1239.8 1.5 copy-start.7
  1241.2 2.9 copy-start.16
  1245.5 1.4 copy-start.24
  1246.3 23.0 %copy-start.10 = (f32[128,32]{0,1:T(8,128)S(1)}, f32[128,32]{0,1:T(8,128)}, u32[]{:S(2)}) copy-start(f32[128,32]{0,1:T(8,128)} %get-tuple-element.188) | copy-start | bytes 49156
  1491.4 2.2 copy-start.3
  1493.6 2.9 copy-start.12
  1497.9 2.5 copy-start.21
  1498.0 2.5 copy-start.20
  1498.0 2.5 copy-start.19
  1498.0 2.5 copy-start.18
  1498.0 2.5 copy-start.17
  (1 other events, 0.7 us)
Sparse Core Ops, SparseCore 0:
  38.0 224.5 all-reduce.22
  295.1 211.6 all-reduce.20
  538.4 216.3 all-reduce.18
  784.4 211.5 all-reduce.16
  1027.5 212.1 all-reduce.14
  1269.5 221.8 all-reduce.12
where the time goes:
time: 1520 us; the launch traced here: 1510 us
  waiting for transfers between devices  1280 us (84%)
  blocking collectives  118 us (8%)
  local copies, waits for them, and re-layouts  33.4 us (2%)
  matrix products  28.8 us (2%)
  other arithmetic  22.2 us (1%)
  between operations  18.9 us (1%)
    psum x6, waiting for transfers between devices, spread(): return lax.psum(block, axis)  1280 us
    all_gather x6, blocking collectives, local(): column_rows = lax.all_gather(owned_rows, 'lev', axis=0, tiled=True)  118 us
  transfers between devices with their start and end apart: 6, of which 6 were waited for; matrix products, arithmetic and copies ran while one was open for 1% of the time, Pallas kernels for 0%

commit v1 on v0

v1 whole, which is shorter than its diff:
```python
import jax, jax.numpy as jnp
from jax import lax
from jax.experimental import pallas as pl
from jax.experimental.pallas import tpu as pltpu
from jax.sharding import PartitionSpec as P
f32 = jnp.float32
bf16 = jnp.bfloat16
HI = lax.Precision.HIGHEST
MESH = pl.DeviceIdType.MESH
X_DIM, Z_DIM, Y_DIM = 4, 8, 8
COLUMNS = X_DIM * Z_DIM * 2
TILE = 128
N, M = 128, 80
PER_LEVEL = 16

def matrices(batches):
    return [(b, None if s == 0 else s - 1) for b in range(batches) for s in range(b + 1)]

def root(q):
    return (q + q // 8) % 4, q % 8, (q // 2) % 2

def rank(x, z, core):
    return (x * Z_DIM + z) * 2 + core

def extract_kernel(obs_cell, state, weights, send):
    batches = obs_cell.shape[0]
    lev = lax.axis_index("lev")
    tiles = weights.shape[1]
    lane = lax.broadcasted_iota(jnp.int32, (M, N), 1)
    for b in range(batches):
        base = b * (b + 1) // 2

        def observation(j, gathered):
            cell = obs_cell[b, lev * PER_LEVEL + j]
            tile, at = cell // TILE, cell % TILE
            chunk = state[pl.ds(tile, M, stride=tiles), :]
            gathered = jnp.where(lane == j, pltpu.roll(chunk, lax.rem(j - at + N, N), 1), gathered)
            for a in range(b):
                send[base + 1 + a, pl.ds(j, 1), :] = weights[a, pl.ds(tile, 1), :]
            return gathered
        gathered = lax.fori_loop(0, PER_LEVEL, observation, jnp.zeros((M, N), f32))
        square = jnp.concatenate([gathered, jnp.zeros((N - M, N), f32)], axis=0)
        send[base] = square.T[:PER_LEVEL]

def extract(obs_cell, state, weights):
    batches = obs_cell.shape[0]
    count = batches * (batches + 1) // 2
    vm = pl.BlockSpec(memory_space=pltpu.VMEM)
    return pl.pallas_call(extract_kernel,
        out_shape=jax.ShapeDtypeStruct((count, PER_LEVEL, N), f32),
        in_specs=[pl.BlockSpec(memory_space=pltpu.SMEM), vm, vm], out_specs=vm,
        compiler_params=pltpu.CompilerParams(vmem_limit_bytes=48 << 20),
    )(obs_cell, state, weights)

def comm_kernel(owner_ids, send, mats, slots, mine, slot_sem, own_sem, push_sem, level_sem, level_push, mat_sem, mat_push):
    count = send.shape[0]
    batches = owner_ids.shape[0]
    h, lev = lax.axis_index("horiz"), lax.axis_index("lev")
    x, z, core = h // (2 * Z_DIM), (h // 2) % Z_DIM, h % 2
    barrier = pltpu.get_barrier_semaphore()
    for step in range(1, COLUMNS):
        pl.semaphore_signal(barrier, inc=1, device_id={"horiz": (h + step) % COLUMNS, "lev": lev}, device_id_type=MESH)
    for step in range(1, Y_DIM):
        pl.semaphore_signal(barrier, inc=1, device_id={"horiz": h, "lev": (lev + step) % Y_DIM}, device_id_type=MESH)
    pl.semaphore_wait(barrier, COLUMNS + Y_DIM - 2)

    which = matrices(batches)
    roots = [rank(*root(q)) for q in range(count)]

    def push(q):
        return pltpu.make_async_remote_copy(send.at[q], slots.at[h], push_sem.at[q], slot_sem,
            device_id={"horiz": roots[q], "lev": lev}, device_id_type=MESH)

    def column(q):
        return pl.ds(pl.multiple_of(lev * PER_LEVEL, PER_LEVEL), PER_LEVEL)

    def level(q, step):
        return pltpu.make_async_remote_copy(mine, mats.at[q, column(q), :], level_push.at[step - 1], level_sem,
            device_id={"horiz": h, "lev": (lev + step) % Y_DIM}, device_id_type=MESH)

    def forward(q, slot, to):
        return pltpu.make_async_remote_copy(mats.at[q], mats.at[q], mat_push.at[q, slot], mat_sem.at[q],
            device_id={"horiz": to, "lev": lev}, device_id_type=MESH)

    def z_peers(q):
        return [(step - 1, rank(x, (z + step) % Z_DIM, core)) for step in range(1, Z_DIM)]

    def x_peers(q):
        return [(6 + step, rank((x + step) % X_DIM, z, core)) for step in range(1, X_DIM)]

    def core_peer(q):
        return [(10, rank(x, z, 1 - core))]

    for q in range(count):
        @pl.when(h != roots[q])
        def _():
            push(q).start()

    for q in range(count):
        @pl.when(h == roots[q])
        def _():
            own = pltpu.make_async_copy(send.at[q], slots.at[h], own_sem)
            own.start()
            own.wait()
            pltpu.make_async_copy(slots.at[1:], slots.at[1:], slot_sem).wait()
            owned = slots[owner_ids[which[q][0]]]
            mine[...] = owned
            for step in range(1, Y_DIM):
                level(q, step).start()
            mats[q, column(q), :] = owned
            for step in range(1, Y_DIM):
                level(q, step).wait_send()
            rows = pl.ds(0, (Y_DIM - 1) * PER_LEVEL)
            pltpu.make_async_copy(mats.at[q, rows, :], mats.at[q, rows, :], level_sem).wait()

    def each(q, then):
        rx, rz, rcore = root(q)
        @pl.when(h == roots[q])
        def _():
            for slot, to in z_peers(q):
                then(forward(q, slot, to))
        @pl.when((x == rx) & (core == rcore))
        def _():
            for slot, to in x_peers(q):
                then(forward(q, slot, to))
        @pl.when(core == rcore)
        def _():
            for slot, to in core_peer(q):
                then(forward(q, slot, to))

    for q in range(count):
        @pl.when(h != roots[q])
        def _():
            pltpu.make_async_copy(mats.at[q], mats.at[q], mat_sem.at[q]).wait()
        each(q, lambda copy: copy.start())
    for q in range(count):
        each(q, lambda copy: copy.wait_send())
        @pl.when(h != roots[q])
        def _():
            push(q).wait_send()

def share(owner_ids, send):
    count = send.shape[0]
    vm = pl.BlockSpec(memory_space=pltpu.VMEM)
    dma = pltpu.SemaphoreType.DMA
    return pl.pallas_call(comm_kernel,
        out_shape=jax.ShapeDtypeStruct((count, N, N), f32),
        in_specs=[pl.BlockSpec(memory_space=pltpu.SMEM), vm], out_specs=vm,
        scratch_shapes=[pltpu.VMEM((COLUMNS, PER_LEVEL, N), f32), pltpu.VMEM((PER_LEVEL, N), f32),
            dma, dma, dma((count,)), dma, dma((Y_DIM - 1,)), dma((count,)), dma((count, 11))],
        compiler_params=pltpu.CompilerParams(vmem_limit_bytes=48 << 20, collective_id=0, has_side_effects=True),
    )(owner_ids, send)

def dot(a, b, ca=1, cb=0, precision=HI):
    return lax.dot_general(a, b, (((ca,), (cb,)), ((), ())), precision=precision, preferred_element_type=f32)

def split3(x):
    h = x.astype(bf16).astype(f32)
    r = x - h
    m = r.astype(bf16).astype(f32)
    return h, m, r - m

def panel_product(left, right):
    h, m, l = split3(left)
    lhs = jnp.concatenate([h, h, m, m, h, l], axis=0).T.astype(bf16)
    h, m, l = split3(right)
    rhs = jnp.concatenate([h, m, h, m, l, h], axis=0).astype(bf16)
    return lax.dot_general(lhs, rhs, (((1,), (0,)), ((), ())), preferred_element_type=f32)

def eliminate(work, solved, root_col):
    row16 = lax.broadcasted_iota(jnp.int32, (16, N), 0)
    row8 = lax.broadcasted_iota(jnp.int32, (8, N), 0)
    lane1 = lax.broadcasted_iota(jnp.int32, (1, N), 1)
    for block in range(N // 8):
        r0 = 8 * block
        tall = 16 if block < N // 8 - 1 else 8
        rows = row16[:tall]
        win_s = work[r0:r0 + tall, 0:N]
        win_a = work[r0:r0 + tall, N:2 * N]
        win_d = work[r0:r0 + tall, 2 * N:3 * N]
        roots = jnp.broadcast_to(root_col[r0:r0 + 8, :], (8, N))
        cols = [jnp.broadcast_to(win_s[:, r0 + k:r0 + k + 1], (tall, N)) for k in range(8)]
        diag = jnp.ones((8, N), f32)
        used_d = jnp.zeros((8, N), f32)
        for j in range(8):
            d = cols[j][j:j + 1, :]
            g = jnp.where(rows > j, cols[j] * (1.0 / d), 0.0)
            for k in range(j + 1, 8):
                cols[k] = cols[k] - g * cols[k][j:j + 1, :]
            win_s = win_s - g * win_s[j:j + 1, :]
            win_a = win_a - g * win_a[j:j + 1, :]
            f = jnp.sqrt(d)
            s = jnp.where(lane1 < M, f / (f + roots[j:j + 1, :]), 1.0)
            scaled = win_d[j:j + 1, :] * s
            win_d = win_d - g * scaled
            diag = jnp.where(row8 == j, d, diag)
            used_d = jnp.where(row8 == j, scaled, used_d)
        if block < N // 8 - 1:
            work[r0 + 8:r0 + 16, 0:N] = win_s[8:]
            work[r0 + 8:r0 + 16, N:2 * N] = win_a[8:]
            work[r0 + 8:r0 + 16, 2 * N:3 * N] = win_d[8:]
        inv = lax.rsqrt(diag)
        f = diag * inv
        solved[r0:r0 + 8, 0:N] = win_a[:8] * inv
        v = jnp.broadcast_to(win_d[:8, M:M + 1], (8, N)) * inv
        solved[r0:r0 + 8, N:2 * N] = jnp.where(lane1 < M, v - win_d[:8] / (f + roots), 0.0)
        if r0 + 16 < N:
            right = jnp.concatenate([win_s[:8], win_a[:8], used_d], axis=1)
            update = panel_product(win_s[:8] / diag, right)
            work[r0 + 16:, :] = work[r0 + 16:, :] - update[r0 + 16:, :]

def chain_kernel(mats, observed, variance, state, local_w, post_out, incs, work, solved, cur, post, state_sem):
    batches = observed.shape[0]
    tiles = state.shape[1]

    def slab(t, outward):
        near, far = post.at[:, t * N:(t + 1) * N], (post_out if outward else state).at[:, t, :]
        return pltpu.make_async_copy(near if outward else far, far if outward else near, state_sem.at[t])
    for t in range(tiles):
        slab(t, False).start()
    lanes = lax.broadcasted_iota(jnp.int32, (N, N), 1)
    eye = lanes == lax.broadcasted_iota(jnp.int32, (N, N), 0)
    member = lanes < M
    for b in range(batches):
        cur[b] = mats[b * (b + 1) // 2]

    def column(row):
        return jnp.sum(jnp.where(eye, row, 0.0), axis=1, keepdims=True)

    def batch(b, _):
        p = cur[b]
        avg = jnp.sum(jnp.where(member, p, 0.0), axis=1, keepdims=True) / M
        dev = jnp.where(member, p - avg, 0.0)
        var_row = variance[pl.ds(b, 1), :]
        var_col = column(var_row)
        obs_col = column(observed[pl.ds(b, 1), :])
        cov = dot(dev, dev, 1, 1) / (M - 1.0)
        work[:, 0:N] = jnp.where(eye, cov + var_row, cov)
        work[:, N:2 * N] = jnp.where(eye, 1.0, 0.0)
        work[:, 2 * N:3 * N] = jnp.where(lanes == M, obs_col - avg, dev)
        eliminate(work, solved, jnp.sqrt(var_col))
        a = solved[:, 0:N]
        m = solved[:, N:2 * N]
        t = dot(a, m, 0, 0)
        sinv = dot(a, a, 0, 0)
        gain = t - dot(sinv, var_col * t)
        incs[b] = dot(t, cov, 0, 1)[:M]

        def later(c, _):
            q = cur[c]
            g = dot(q, dev, 1, 1) * mats[c * (c + 1) // 2 + 1 + b] * (1.0 / (M - 1.0))
            cur[c] = q + dot(g, gain)
            return 0
        lax.fori_loop(b + 1, batches, later, 0)

        dev_m = dev[:, :M]
        gain_m = gain[:, :M]
        dh = dev_m.astype(bf16); dl = (dev_m - dh.astype(f32)).astype(bf16)
        dcat = jnp.concatenate([dh, dl, dh], axis=1)
        gt = gain.T[:M] * (1.0 / (M - 1.0))
        gh = gt.astype(bf16); gl = (gt - gh.astype(f32)).astype(bf16)
        gcat = jnp.concatenate([gh, gl, gh], axis=1)
        weights = local_w[b].T
        @pl.when(b == 0)
        def _():
            for t in range(tiles):
                slab(t, False).wait()
        for chunk in range(8):
            cs = 512 * chunk
            x = post[:, cs:cs + 512]
            xh = x.astype(bf16); xl = (x - xh.astype(f32)).astype(bf16)
            xcat = jnp.concatenate([xh, xh, xl], axis=0)
            r = dot(dcat, xcat, precision=None)
            scale = jnp.concatenate([jnp.broadcast_to(weights[:, t:t + 1], (N, N)) for t in range(4 * chunk, 4 * chunk + 4)], axis=1)
            r = r * scale
            rh = r.astype(bf16); rl = (r - rh.astype(f32)).astype(bf16)
            rcat = jnp.concatenate([rh, rh, rl], axis=0)
            post[:, cs:cs + 512] = x + dot(gcat, rcat, precision=None)
        return 0
    lax.fori_loop(0, batches, batch, 0)
    for t in range(tiles):
        slab(t, True).start()
    for t in range(tiles):
        slab(t, True).wait()

def chain(mats, observed, variance, state, local_w):
    batches = observed.shape[0]
    vm = pl.BlockSpec(memory_space=pltpu.VMEM)
    return pl.pallas_call(chain_kernel,
        out_shape=(jax.ShapeDtypeStruct(state.shape, f32), jax.ShapeDtypeStruct((batches, M, N), f32)),
        in_specs=[vm] * 3 + [pl.BlockSpec(memory_space=pl.ANY), vm], out_specs=(pl.BlockSpec(memory_space=pl.ANY), vm),
        scratch_shapes=[pltpu.VMEM((N, 3 * N), f32), pltpu.VMEM((N, 2 * N), f32), pltpu.VMEM((batches, N, N), f32),
            pltpu.VMEM((M, state.shape[1] * N), f32), pltpu.SemaphoreType.DMA((state.shape[1],))],
        compiler_params=pltpu.CompilerParams(vmem_limit_bytes=48 << 20),
        cost_estimate=pl.CostEstimate(flops=10**9, bytes_accessed=4 * 10**6, transcendentals=0),
    )(mats, observed, variance, state, local_w)


def local(prior_state, localization, observed, error_variance, owner_ids, obs_cell):
    members, _, cells = prior_state.shape
    tiles = cells // TILE
    batches = obs_cell.shape[0]
    weights = jnp.transpose(localization.reshape(batches, N, tiles), (0, 2, 1))
    send = extract(obs_cell, prior_state.reshape(members * tiles, TILE), weights)
    mats = share(owner_ids, send)
    state, increments = chain(mats, observed, error_variance, prior_state.reshape(members, tiles, TILE), weights)
    return state.reshape(members, 1, cells), jnp.transpose(increments, (0, 2, 1))


def solution(mesh):
    in_specs = (P(None, "lev", "horiz"), P(None, None, "lev", "horiz"), P(), P(), P(), P())
    out_specs = (P(None, "lev", "horiz"), P())
    return jax.shard_map(local, mesh=mesh, in_specs=in_specs, out_specs=out_specs, check_vma=False)
```

time: 1520 us -> 247 us (0.16)
  waiting for transfers between devices: 1280 us -> 0 us
  Pallas kernels: 0 us -> 243 us
  blocking collectives: 118 us -> 0 us
  local copies, waits for them, and re-layouts: 33.4 us -> 2.91 us
  matrix products: 28.8 us -> 0 us
  other arithmetic: 22.2 us -> 0 us
  between operations: 18.9 us -> 0.86 us
    psum x6 -> x0, waiting for transfers between devices: 1280 us -> none  [spread(): return lax.psum(block, axis)]
    pallas_call x0 -> x3, Pallas kernels: none -> 243 us  [the longest x1 174 us: share(): pl.pallas_call(comm_kernel, out_shape=jax.ShapeDtypeStruct((count, N, N),...]
    all_gather x6 -> x0, blocking collectives: 118 us -> none  [local(): column_rows = lax.all_gather(owned_rows, 'lev', axis=0, tiled=True)]
    dot_general x12 -> x0, matrix products: 28.8 us -> none  [the longest x6 19.1 us: regress(): covariance = jnp.dot(deviation, current, precision=highest)]
  transfers between devices with their start and end apart: 6 -> 0, of which waited for: 6 -> 0; matrix products, arithmetic and copies ran while one was open for 1% -> 0% of each run, Pallas kernels for 0% -> 0%
where the time goes in v1:
time: 247 us; the launch traced here: 246 us
  Pallas kernels  243 us (98%)
  local copies, waits for them, and re-layouts  2.91 us (1%)
    pallas_call x1, Pallas kernels, share(): pl.pallas_call(comm_kernel, out_shape=jax.ShapeDtypeStruct((count, N, N),...  174 us
    pallas_call x1, Pallas kernels, chain(): pl.pallas_call(chain_kernel, out_shape=(jax.ShapeDtypeStruct(state.shape,...  57 us
    pallas_call x1, Pallas kernels, extract(): pl.pallas_call(extract_kernel, out_shape=jax.ShapeDtypeStruct((count, PER...  11.9 us

profile of v1, /device:TPU:1, one launch (start us, length us, event | category | flops | bytes accessed | tf_op | source)
XLA Modules:
  0.0 246.5 jit_solution(7154501973760323682)
XLA Ops:
  0.6 0.0 copy-start.5
  0.6 0.0 copy-start
  0.7 1.3 copy-done
  2.0 0.0 copy-start.2
  2.0 0.9 copy-done.2
  2.9 0.0 copy-start.4
  2.9 0.7 copy-done.4
  3.5 0.0 copy-start.1
  3.5 0.0 copy-start.3
  3.5 0.0 copy-start.6
  3.6 0.0 copy-start.7
  3.6 11.9 %shard_map.77.send = f32[21,16,128]{2,1,0:T(8,128)S(1)} custom-call(s32[6,128]{1,0:T(8,128)S(1)} %copy-done.4, f32[2560,128]{1,0:T(8,128)S(1)} %bitcast.7, f32[6,32,128]{2,1,0:T(8,128)S(1)} %bitcast.9), custom_call_target="tpu_custom_call" | custom-call | tf_op jit(solution)/shard_map/pallas_call | solution.py:49
  15.4 0.0 copy-done.5
  15.4 173.9 %shard_map.78.mats = f32[21,128,128]{2,1,0:T(8,128)S(1)} custom-call(s32[6]{0:T(128)S(1)} %copy-done.5, f32[21,16,128]{2,1,0:T(8,128)S(1)} %shard_map.77.send), custom_call_target="tpu_custom_call" | custom-call | tf_op jit(solution)/shard_map/pallas_call | solution.py:146
  189.3 0.0 copy-done.1
  189.3 0.0 copy-done.3
  189.3 0.0 copy-done.6
  189.3 0.0 copy-done.7
  189.4 57.0 %shard_map.79 = (f32[80,32,128]{2,1,0:T(8,128)}, f32[6,80,128]{2,1,0:T(8,128)}) custom-call(f32[21,128,128]{2,1,0:T(8,128)S(1)} %shard_map.78.mats, f32[6,128]{1,0:T(8,128)S(1)} %copy-done.6, f32[6,128]{1,0:T(8,128)S(1)} %copy-done.7, f32[80,32,128]{2,1,0:T(8,128)S(1)} %bitcast.8, f32[6,32,128]{2,1,0:T(8,128)S(1)} %bitcast.10), custom_call_target="tpu_custom_call" | custom-call | flops 1000000000 | bytes 4000000 | tf_op jit(solution)/shard_map/pallas_call | solution.py:289
Async XLA Ops:
  0.6 14.8 %copy-start.5 = (s32[6]{0:T(128)S(1)}, s32[6]{0:T(128)}, u32[]{:S(2)}) copy-start(s32[6]{0:T(128)} %owner_ids.1) | copy-start | bytes 76
  0.6 1.3 copy-start
  2.0 0.9 copy-start.2
  2.9 0.7 copy-start.4
  3.5 185.8 %copy-start.1 = (f32[80,1,4096]{2,1,0:T(1,128)S(1)}, f32[80,1,4096]{2,1,0:T(1,128)}, u32[]{:S(2)}) copy-start(f32[80,1,4096]{2,1,0:T(1,128)} %param.6) | copy-start | bytes 3932164
  3.5 185.8 %copy-start.3 = (f32[6,128,1,32]{1,3,2,0:T(8,128)S(1)}, f32[6,128,1,32]{1,3,2,0:T(8,128)}, u32[]{:S(2)}) copy-start(f32[6,128,1,32]{1,3,2,0:T(8,128)} %param.7) | copy-start | bytes 294916
  3.5 185.8 %copy-start.6 = (f32[6,128]{1,0:T(8,128)S(1)}, f32[6,128]{1,0:T(8,128)}, u32[]{:S(2)}) copy-start(f32[6,128]{1,0:T(8,128)} %observed.1) | copy-start | bytes 9220
  3.6 185.8 %copy-start.7 = (f32[6,128]{1,0:T(8,128)S(1)}, f32[6,128]{1,0:T(8,128)}, u32[]{:S(2)}) copy-start(f32[6,128]{1,0:T(8,128)} %variance.1) | copy-start | bytes 9220

commit v2 on v1

v2 whole, which is shorter than its diff:
```python
import jax
import jax.numpy as jnp
from jax import lax
from jax.experimental import pallas as pl
from jax.experimental.pallas import tpu as pltpu
from jax.sharding import PartitionSpec as P

f32 = jnp.float32
bf16 = jnp.bfloat16
HI = lax.Precision.HIGHEST
MESH = pl.DeviceIdType.MESH
X_DIM, Z_DIM, Y_DIM = 4, 8, 8
TILE = 128
N, M = 128, 80
PER_LEVEL = N // Y_DIM


def dot(a, b, ca=1, cb=0, precision=HI):
    return lax.dot_general(a, b, (((ca,), (cb,)), ((), ())), precision=precision, preferred_element_type=f32)


def split3(x):
    h = x.astype(bf16).astype(f32)
    r = x - h
    m = r.astype(bf16).astype(f32)
    return h, m, r - m


def panel_product(left, right):
    h, m, l = split3(left)
    lhs = jnp.concatenate([h, h, m, m, h, l], axis=0).T.astype(bf16)
    h, m, l = split3(right)
    rhs = jnp.concatenate([h, m, h, m, l, h], axis=0).astype(bf16)
    return lax.dot_general(lhs, rhs, (((1,), (0,)), ((), ())), preferred_element_type=f32)


def eliminate(work, solved, root_col):
    row16 = lax.broadcasted_iota(jnp.int32, (16, N), 0)
    row8 = lax.broadcasted_iota(jnp.int32, (8, N), 0)
    lane1 = lax.broadcasted_iota(jnp.int32, (1, N), 1)
    for block in range(N // 8):
        r0 = 8 * block
        tall = 16 if block < N // 8 - 1 else 8
        rows = row16[:tall]
        win_s = work[r0:r0 + tall, 0:N]
        win_a = work[r0:r0 + tall, N:2 * N]
        win_d = work[r0:r0 + tall, 2 * N:3 * N]
        roots = jnp.broadcast_to(root_col[r0:r0 + 8, :], (8, N))
        cols = [jnp.broadcast_to(win_s[:, r0 + k:r0 + k + 1], (tall, N)) for k in range(8)]
        diag = jnp.ones((8, N), f32)
        used_d = jnp.zeros((8, N), f32)
        for j in range(8):
            d = cols[j][j:j + 1, :]
            g = jnp.where(rows > j, cols[j] * (1.0 / d), 0.0)
            for k in range(j + 1, 8):
                cols[k] = cols[k] - g * cols[k][j:j + 1, :]
            win_s = win_s - g * win_s[j:j + 1, :]
            win_a = win_a - g * win_a[j:j + 1, :]
            f = jnp.sqrt(d)
            s = jnp.where(lane1 < M, f / (f + roots[j:j + 1, :]), 1.0)
            scaled = win_d[j:j + 1, :] * s
            win_d = win_d - g * scaled
            diag = jnp.where(row8 == j, d, diag)
            used_d = jnp.where(row8 == j, scaled, used_d)
        if block < N // 8 - 1:
            work[r0 + 8:r0 + 16, 0:N] = win_s[8:]
            work[r0 + 8:r0 + 16, N:2 * N] = win_a[8:]
            work[r0 + 8:r0 + 16, 2 * N:3 * N] = win_d[8:]
        inv = lax.rsqrt(diag)
        f = diag * inv
        solved[r0:r0 + 8, 0:N] = win_a[:8] * inv
        v = jnp.broadcast_to(win_d[:8, M:M + 1], (8, N)) * inv
        solved[r0:r0 + 8, N:2 * N] = jnp.where(lane1 < M, v - win_d[:8] / (f + roots), 0.0)
        if r0 + 16 < N:
            right = jnp.concatenate([win_s[:8], win_a[:8], used_d], axis=1)
            update = panel_product(win_s[:8] / diag, right)
            work[r0 + 16:, :] = work[r0 + 16:, :] - update[r0 + 16:, :]


def first(b):
    return b * (b + 1) // 2


def rank(x, z, core):
    return (x * Z_DIM + z) * 2 + core


def kernel(owner_ids, send, observed, variance, state, weights, post_out, incs, *scratch):
    batches = observed.shape[0]
    tiles = state.shape[1]
    near = scratch[0:batches]
    line = scratch[batches:2 * batches]
    picked = scratch[2 * batches:3 * batches]
    mats, cur, devs, gains, work, solved, post, local_w, state_sem, weight_sem, push, arrive = scratch[3 * batches:]
    h, lev = lax.axis_index("horiz"), lax.axis_index("lev")
    x, z, core = h // (2 * Z_DIM), (h // 2) % Z_DIM, h % 2
    lanes = lax.broadcasted_iota(jnp.int32, (N, N), 1)
    eye = lanes == lax.broadcasted_iota(jnp.int32, (N, N), 0)
    member = lanes < M

    near_peers = [rank((x + s) % X_DIM, z, (core + c) % 2) for s in range(X_DIM) for c in range(2) if s or c]
    near_peers = [{"horiz": to, "lev": lev} for to in near_peers]
    line_peers = [{"horiz": rank(x, (z + s) % Z_DIM, core), "lev": lev} for s in range(1, Z_DIM)]
    level_peers = [{"horiz": h, "lev": (lev + s) % Y_DIM} for s in range(1, Y_DIM)]
    peers = [near_peers, line_peers, level_peers]

    barrier = pltpu.get_barrier_semaphore()
    for to in near_peers + line_peers + level_peers:
        pl.semaphore_signal(barrier, inc=1, device_id=to, device_id_type=MESH)

    def slab(t, outward):
        inside, far = post.at[:, t * N:(t + 1) * N], (post_out if outward else state).at[:, t, :]
        return pltpu.make_async_copy(inside if outward else far, far if outward else inside, state_sem.at[t])
    for t in range(tiles):
        slab(t, False).start()
    fetch = pltpu.make_async_copy(weights, local_w, weight_sem)
    fetch.start()
    def copies(b, stage):
        if stage == 0:
            source, target = send.at[first(b):first(b + 1)], near[b].at[x * 2 + core]
        elif stage == 1:
            source, target = picked[b], line[b].at[z]
        else:
            source, target = line[b].at[Z_DIM], mats.at[first(b):first(b + 1), lev]
        return [
            pltpu.make_async_remote_copy(source, target, push.at[b, stage, i], arrive.at[b, stage], device_id=to, device_id_type=MESH)
            for i, to in enumerate(peers[stage])
        ]

    def start(b, stage):
        owner = owner_ids[b]
        if stage == 0:
            near[b][x * 2 + core] = send[first(b):first(b + 1)]
        elif stage == 1:
            block = near[b][(owner // (2 * Z_DIM)) * 2 + owner % 2]
            picked[b][...] = block
            line[b][z] = block
        else:
            block = line[b][(owner // 2) % Z_DIM]
            line[b][Z_DIM] = block
            mats[first(b):first(b + 1), lev] = block
        for copy in copies(b, stage):
            copy.start()

    def arrived(b, stage):
        count = len(peers[stage])
        whole = [near[b].at[0:count], line[b].at[0:count], mats.at[first(b):first(b + 1), 0:count]][stage]
        pltpu.make_async_copy(whole, whole, arrive.at[b, stage]).wait()

    pl.semaphore_wait(barrier, len(near_peers) + len(line_peers) + len(level_peers))
    start(0, 0)
    start(1, 0)
    arrived(0, 0)
    start(0, 1)
    arrived(1, 0)
    start(1, 1)
    start(2, 0)
    arrived(0, 1)
    start(0, 2)
    arrived(1, 1)
    start(1, 2)
    arrived(2, 0)
    start(2, 1)
    start(3, 0)
    arrived(0, 2)

    for t in range(tiles):
        slab(t, False).wait()
    fetch.wait()

    def service(b):
        if b + 2 < batches:
            arrived(b + 2, 1)
            start(b + 2, 2)
        if b + 3 < batches:
            arrived(b + 3, 0)
            start(b + 3, 1)
        if b + 4 < batches:
            start(b + 4, 0)

    def column(row):
        return jnp.sum(jnp.where(eye, row, 0.0), axis=1, keepdims=True)

    def carry_over(c, a):
        q = cur[c]
        g = dot(q, devs[a], 1, 1) * mats[c * (c + 1) // 2 + 1 + a].reshape(N, N) * (1.0 / (M - 1.0))
        cur[c] = q + dot(g, gains[a])

    cur[0] = mats[0].reshape(N, N)

    def batch(b, _):
        p = cur[b]
        avg = jnp.sum(jnp.where(member, p, 0.0), axis=1, keepdims=True) / M
        dev = jnp.where(member, p - avg, 0.0)
        devs[b] = dev
        var_row = variance[pl.ds(b, 1), :]
        var_col = column(var_row)
        obs_col = column(observed[pl.ds(b, 1), :])
        cov = dot(dev, dev, 1, 1) / (M - 1.0)
        work[:, 0:N] = jnp.where(eye, cov + var_row, cov)
        work[:, N:2 * N] = jnp.where(eye, 1.0, 0.0)
        work[:, 2 * N:3 * N] = jnp.where(lanes == M, obs_col - avg, dev)
        eliminate(work, solved, jnp.sqrt(var_col))
        for k in range(batches):
            @pl.when(b == k)
            def _():
                service(k)
        a = solved[:, 0:N]
        m = solved[:, N:2 * N]
        t = dot(a, m, 0, 0)
        sinv = dot(a, a, 0, 0)
        gain = t - dot(sinv, var_col * t)
        gains[b] = gain
        incs[b] = dot(t, cov, 0, 1)[:M]

        for k in range(batches - 1):
            @pl.when(b == k)
            def _():
                arrived(k + 1, 2)
                cur[k + 1] = mats[first(k + 1)].reshape(N, N)

        @pl.when(b < batches - 1)
        def _():
            def past(a, _):
                carry_over(b + 1, a)
                return 0
            lax.fori_loop(0, b + 1, past, 0)

        dev_m = dev[:, :M]
        dh = dev_m.astype(bf16)
        dl = (dev_m - dh.astype(f32)).astype(bf16)
        dcat = jnp.concatenate([dh, dl, dh], axis=1)
        gt = gain.T[:M] * (1.0 / (M - 1.0))
        gh = gt.astype(bf16)
        gl = (gt - gh.astype(f32)).astype(bf16)
        gcat = jnp.concatenate([gh, gl, gh], axis=1)
        scales = local_w[b].T
        for chunk in range(tiles // 4):
            cs = 512 * chunk
            old = post[:, cs:cs + 512]
            xh = old.astype(bf16)
            xl = (old - xh.astype(f32)).astype(bf16)
            r = dot(dcat, jnp.concatenate([xh, xh, xl], axis=0), precision=None)
            scale = [jnp.broadcast_to(scales[:, t:t + 1], (N, N)) for t in range(4 * chunk, 4 * chunk + 4)]
            r = r * jnp.concatenate(scale, axis=1)
            rh = r.astype(bf16)
            rl = (r - rh.astype(f32)).astype(bf16)
            post[:, cs:cs + 512] = old + dot(gcat, jnp.concatenate([rh, rh, rl], axis=0), precision=None)
        return 0
    lax.fori_loop(0, batches, batch, 0)

    for t in range(tiles):
        slab(t, True).start()
    for b in range(batches):
        for stage in range(3):
            for copy in copies(b, stage):
                copy.wait_send()
    for t in range(tiles):
        slab(t, True).wait()


def extract_kernel(obs_cell, state, weights, send):
    batches, tiles = weights.shape[0], weights.shape[1]
    lev = lax.axis_index("lev")
    lane = lax.broadcasted_iota(jnp.int32, (M, N), 1)
    for b in range(batches):
        gathered = jnp.zeros((M, N), f32)
        for j in range(PER_LEVEL):
            cell = obs_cell[b, lev * PER_LEVEL + j]
            tile, at = cell // TILE, cell % TILE
            chunk = state[pl.ds(tile, M, stride=tiles), :]
            gathered = jnp.where(lane == j, pltpu.roll(chunk, lax.rem(j - at + N, N), 1), gathered)
            for a in range(b):
                send[first(b) + 1 + a, j:j + 1, :] = weights[a, pl.ds(tile, 1), :]
        square = jnp.concatenate([gathered, jnp.zeros((N - M, N), f32)], axis=0)
        send[first(b)] = square.T[:PER_LEVEL]


def extract(obs_cell, state, weights):
    vm = pl.BlockSpec(memory_space=pltpu.VMEM)
    return pl.pallas_call(
        extract_kernel,
        out_shape=jax.ShapeDtypeStruct((first(obs_cell.shape[0]), PER_LEVEL, N), f32),
        in_specs=[pl.BlockSpec(memory_space=pltpu.SMEM), vm, vm],
        out_specs=vm,
        compiler_params=pltpu.CompilerParams(vmem_limit_bytes=48 << 20),
    )(obs_cell, state, weights)


def assimilate(owner_ids, send, observed, variance, state, weights):
    batches = observed.shape[0]
    tiles = state.shape[1]
    vm = pl.BlockSpec(memory_space=pltpu.VMEM)
    smem = pl.BlockSpec(memory_space=pltpu.SMEM)
    hbm = pl.BlockSpec(memory_space=pl.ANY)
    dma = pltpu.SemaphoreType.DMA

    def block(*lead):
        return pltpu.VMEM((*lead, N), f32)
    count = first(batches)
    groups = [(b + 1, PER_LEVEL) for b in range(batches)]
    return pl.pallas_call(
        kernel,
        out_shape=(jax.ShapeDtypeStruct(state.shape, f32), jax.ShapeDtypeStruct((batches, M, N), f32)),
        in_specs=[smem, vm, vm, vm, hbm, hbm],
        out_specs=(hbm, vm),
        scratch_shapes=[block(2 * X_DIM, *g) for g in groups] + [block(Z_DIM + 1, *g) for g in groups] + [block(*g) for g in groups] + [
            block(count, Y_DIM, PER_LEVEL), block(batches, N), block(batches, N), block(batches, N),
            pltpu.VMEM((N, 3 * N), f32), pltpu.VMEM((N, 2 * N), f32), pltpu.VMEM((M, tiles * N), f32), block(batches, tiles),
            dma((tiles,)), dma, dma((batches, 3, max(2 * X_DIM, Z_DIM, Y_DIM) - 1)), dma((batches, 3)),
        ],
        compiler_params=pltpu.CompilerParams(vmem_limit_bytes=48 << 20, collective_id=0, has_side_effects=True),
        cost_estimate=pl.CostEstimate(flops=10**9, bytes_accessed=4 * 10**6, transcendentals=0),
    )(owner_ids, send, observed, variance, state, weights)


def local(prior_state, localization, observed, error_variance, owner_ids, obs_cell):
    members, _, cells = prior_state.shape
    tiles = cells // TILE
    batches = obs_cell.shape[0]
    weights = jnp.transpose(localization.reshape(batches, N, tiles), (0, 2, 1))
    send = extract(obs_cell, prior_state.reshape(members * tiles, TILE), weights)
    state, increments = assimilate(owner_ids, send, observed, error_variance, prior_state.reshape(members, tiles, TILE), weights)
    return state.reshape(members, 1, cells), jnp.transpose(increments, (0, 2, 1))


def solution(mesh):
    in_specs = (P(None, "lev", "horiz"), P(None, None, "lev", "horiz"), P(), P(), P(), P())
    out_specs = (P(None, "lev", "horiz"), P())
    return jax.shard_map(local, mesh=mesh, in_specs=in_specs, out_specs=out_specs, check_vma=False)
```

time: 247 us -> 99.6 us (0.40)
  the two profiles are of different devices: /device:TPU:1 before, /device:TPU:2 now
where the time goes in v2:
time: 99.6 us; the launch traced here: 99.4 us
  Pallas kernels  94 us (94%)
  local copies, waits for them, and re-layouts  4.67 us (5%)
    pallas_call x1, Pallas kernels, assimilate(): pl.pallas_call(kernel, out_shape=(jax.ShapeDtypeStruct(state.shape, f32),...  89 us
    pallas_call x1, Pallas kernels, extract(): pl.pallas_call(extract_kernel, out_shape=jax.ShapeDtypeStruct((first(obs_...  5.05 us
    unnamed x16, local copies, waits for them, and re-layouts  4.67 us

profile of v2, /device:TPU:2, one launch (start us, length us, event | category | flops | bytes accessed | tf_op | source)
XLA Modules:
  0.0 99.4 jit_solution(5489918214692984403)
XLA Ops:
  0.6 0.0 copy-start.6
  0.6 0.0 copy-start.4
  0.7 0.0 copy-start
  0.7 1.3 %copy-done = f32[80,1,4096]{2,1,0:T(1,128)S(1)} copy-done((f32[80,1,4096]{2,1,0:T(1,128)S(1)}, f32[80,1,4096]{2,1,0:T(1,128)}, u32[]{:S(2)}) %copy-start) | copy-done | bytes 1310744
  2.0 0.0 copy-start.2
  2.0 0.9 copy-done.2
  2.9 0.0 copy-start.3
  2.9 0.7 copy-done.3
  3.6 0.0 copy-start.1
  3.6 0.0 copy-start.5
  3.6 5.1 %shard_map.77.send = f32[21,16,128]{2,1,0:T(8,128)S(1)} custom-call(s32[6,128]{1,0:T(8,128)S(1)} %copy-done.3, f32[2560,128]{1,0:T(8,128)S(1)} %bitcast.7, f32[6,32,128]{2,1,0:T(8,128)S(1)} %bitcast.11), custom_call_target="tpu_custom_call" | custom-call | tf_op jit(solution)/shard_map/pallas_call | solution.py:281
  8.6 0.0 copy-done.6
  8.6 0.0 copy-done.4
  8.6 0.0 copy-done.1
  8.6 0.0 copy-done.5
  8.6 89.0 %shard_map.78 = (f32[80,32,128]{2,1,0:T(8,128)S(1)}, f32[6,80,128]{2,1,0:T(8,128)S(1)}) custom-call(s32[6]{0:T(128)S(1)} %copy-done.6, f32[21,16,128]{2,1,0:T(8,128)S(1)} %shard_map.77.send, f32[6,128]{1,0:T(8,128)S(1)} %copy-done.4, f32[6,128]{1,0:T(8,128)S(1)} %copy-done.5, f32[80,32,128]{2,1,0:T(8,128)S(1)} %bitcast.8, f32[6,32,128]{2,1,0:T(8,128)S(1)} %bitcast.12), custom_call_target="tpu_custom_call" | custom-call | flops 1000000000 | bytes 4000000 | tf_op jit(solution)/shard_map/pallas_call | solution.py:302
  97.6 1.1 %copy.11 = f32[80,1,4096]{2,1,0:T(1,128)} copy(f32[80,1,4096]{2,1,0:T(1,128)S(1)} %bitcast.9) | data formatting | bytes 2621440
  98.7 0.7 copy.12
Async XLA Ops:
  0.6 8.0 %copy-start.6 = (s32[6]{0:T(128)S(1)}, s32[6]{0:T(128)}, u32[]{:S(2)}) copy-start(s32[6]{0:T(128)} %owner_ids.1) | copy-start | bytes 76
  0.6 8.0 %copy-start.4 = (f32[6,128]{1,0:T(8,128)S(1)}, f32[6,128]{1,0:T(8,128)}, u32[]{:S(2)}) copy-start(f32[6,128]{1,0:T(8,128)} %observed.1) | copy-start | bytes 9220
  0.7 1.3 %copy-start = (f32[80,1,4096]{2,1,0:T(1,128)S(1)}, f32[80,1,4096]{2,1,0:T(1,128)}, u32[]{:S(2)}) copy-start(f32[80,1,4096]{2,1,0:T(1,128)} %param.6) | copy-start | bytes 3932164
  2.0 0.9 copy-start.2
  2.9 0.7 copy-start.3
  3.6 5.1 %copy-start.1 = (f32[80,1,4096]{2,1,0:T(1,128)S(1)}, f32[80,1,4096]{2,1,0:T(1,128)}, u32[]{:S(2)}) copy-start(f32[80,1,4096]{2,1,0:T(1,128)} %param.6) | copy-start | bytes 3932164
  3.6 5.1 %copy-start.5 = (f32[6,128]{1,0:T(8,128)S(1)}, f32[6,128]{1,0:T(8,128)}, u32[]{:S(2)}) copy-start(f32[6,128]{1,0:T(8,128)} %variance.1) | copy-start | bytes 9220

commit v3 on v2

v3 whole, which is shorter than its diff:
```python
import jax
import jax.numpy as jnp
from jax import lax
from jax.experimental import pallas as pl
from jax.experimental.pallas import tpu as pltpu
from jax.sharding import PartitionSpec as P

f32 = jnp.float32
bf16 = jnp.bfloat16
HI = lax.Precision.HIGHEST
MESH = pl.DeviceIdType.MESH
X_DIM, Z_DIM, Y_DIM = 4, 8, 8
TILE = 128
N, M = 128, 80
PER_LEVEL = N // Y_DIM
WHOLE_GROUPS = 2
ARRIVAL = (7, 5, 3, 3, 3)
SERVICES = {
    0: {0: [(3, 1)], 4: [(2, 2), (5, 0), (4, 1)]},
    1: {0: [(3, 2), (5, 1)], 3: [(2, 3)], 4: [(4, 2)], 7: [(3, 3)]},
    2: {0: [(5, 2)], 4: [(4, 3)]},
    3: {1: [(5, 3)]},
}


def dot(a, b, ca=1, cb=0, precision=HI):
    return lax.dot_general(a, b, (((ca,), (cb,)), ((), ())), precision=precision, preferred_element_type=f32)


def split3(x):
    h = x.astype(bf16).astype(f32)
    r = x - h
    m = r.astype(bf16).astype(f32)
    return h, m, r - m


def panel_product(left, right):
    h, m, l = split3(left)
    lhs = jnp.concatenate([h, h, m, m, h, l], axis=0).T.astype(bf16)
    h, m, l = split3(right)
    rhs = jnp.concatenate([h, m, h, m, l, h], axis=0).astype(bf16)
    return lax.dot_general(lhs, rhs, (((1,), (0,)), ((), ())), preferred_element_type=f32)


BLOCK = 16


def lane_copy(tile, lane):
    return jnp.take_along_axis(tile, jnp.full(tile.shape, lane, jnp.int32), axis=1)


def row_copy(tile, row):
    return jnp.broadcast_to(tile[row:row + 1], tile.shape)


def eliminate(work, sums, root_col, beside):
    row8 = lax.broadcasted_iota(jnp.int32, (8, N), 0)
    lane8 = lax.broadcasted_iota(jnp.int32, (8, N), 1)
    own = BLOCK // 8
    for r0 in range(0, N, BLOCK):
        tall = min(2 * BLOCK, N - r0) // 8
        inside = (lane8 >= r0) & (lane8 < r0 + BLOCK)
        win_s = [work[r0 + 8 * t:r0 + 8 * t + 8, 0:N] for t in range(tall)]
        win_d = [work[r0 + 8 * t:r0 + 8 * t + 8, N:2 * N] for t in range(tall)]
        roots = [jnp.broadcast_to(root_col[r0 + 8 * t:r0 + 8 * t + 8, :], (8, N)) for t in range(own)]
        cols = [[lane_copy(w, r0 + k) for w in win_s] for k in range(BLOCK)]
        win_s = [jnp.where(inside, jnp.where(lane8 == row8 + (r0 + 8 * t), 1.0, 0.0) if t < own else 0.0, w) for t, w in enumerate(win_s)]
        diag = [jnp.ones((8, N), f32)] * own
        unit = []
        for j in range(0, BLOCK, 2):
            i = j + 1
            home, sj, si = j // 8, j % 8, j % 8 + 1
            cj, ci = cols[j], cols[i]
            a, b, e = row_copy(cj[home], sj), row_copy(cj[home], si), row_copy(ci[home], si)
            det = a * e - b * b
            idet = 1.0 / det
            p, q, r = e * idet, b * idet, a * idet
            ia = 1.0 / a
            ratio = b * ia
            diag[home] = jnp.where(row8 == sj, a, jnp.where(row8 == si, det * ia, diag[home]))
            row_sj, row_si = row_copy(win_s[home], sj), row_copy(win_s[home], si)
            cols_j = {k: row_copy(cols[k][home], sj) for k in range(i + 1, BLOCK)}
            cols_i = {k: row_copy(cols[k][home], si) for k in range(i + 1, BLOCK)}
            unit_j, unit_i = {}, {}
            for t in range(home, tall):
                gj = cj[t] * p - ci[t] * q
                gi = ci[t] * r - cj[t] * q
                gd = cj[t] * ia
                if t == home:
                    below = row8 > si
                    gj, gi = jnp.where(below, gj, 0.0), jnp.where(below, gi, 0.0)
                    gd = jnp.where(row8 > sj, gd, 0.0)
                unit_j[t], unit_i[t] = gd, gi
                if not (t == home and si == 7):
                    for k in range(i + 1, BLOCK):
                        cols[k][t] = cols[k][t] - gj * cols_j[k] - gi * cols_i[k]
                if t == home:
                    gj = jnp.where(row8 == si, ratio, gj)
                win_s[t] = win_s[t] - gj * row_sj - gi * row_si
            unit += [unit_j, unit_i]
        inv = [lax.rsqrt(d) for d in diag]
        f = [d * v for d, v in zip(diag, inv)]
        shrink = [jnp.where(lane8 < M, f[t] / (f[t] + roots[t]), 1.0) for t in range(own)]
        for j in range(BLOCK):
            home = j // 8
            scaled = row_copy(win_d[home] * shrink[home], j % 8)
            for t in unit[j]:
                win_d[t] = win_d[t] - unit[j][t] * scaled
        for t in range(own, tall):
            work[r0 + 8 * t:r0 + 8 * t + 8, 0:N] = win_s[t]
            work[r0 + 8 * t:r0 + 8 * t + 8, N:2 * N] = win_d[t]
        block_s = jnp.concatenate(win_s[:own], axis=0)
        low = r0 + 2 * BLOCK
        if low < N:
            left = jnp.concatenate([win_s[t] / diag[t] for t in range(own)], axis=0)
            right = jnp.concatenate([block_s, jnp.concatenate([win_d[t] * shrink[t] for t in range(own)], axis=0)], axis=1)
            update = panel_product(left, right)
            old = work[low:, 0:N]
            gone = lax.broadcasted_iota(jnp.int32, old.shape, 1)
            work[low:, 0:N] = jnp.where((gone >= r0) & (gone < r0 + BLOCK), 0.0, old) - update[low:, 0:N]
            work[low:, N:2 * N] = work[low:, N:2 * N] - update[low:, N:2 * N]
        a = jnp.concatenate([jnp.where(lane8 < r0 + BLOCK, win_s[t] * inv[t], 0.0) for t in range(own)], axis=0)
        m = jnp.concatenate([win_d[t] * jnp.where(lane8 < M, -1.0 / (f[t] + roots[t]), inv[t]) for t in range(own)], axis=0)
        update = panel_product(a, jnp.concatenate([a, m], axis=1))
        if r0 == 0:
            sums[...] = update
        else:
            sums[0:r0 + BLOCK, :] = sums[0:r0 + BLOCK, :] + update[0:r0 + BLOCK]
        beside(r0 // BLOCK)


def first(b):
    return b * (b + 1) // 2


def rank(x, z, core):
    return (x * Z_DIM + z) * 2 + core


def kernel(owner_ids, send, observed, variance, state, weights, post_out, incs, *scratch):
    batches = observed.shape[0]
    tiles = state.shape[1]
    near = scratch[0:batches]
    line = scratch[batches:2 * batches]
    picked = scratch[2 * batches:3 * batches]
    (mats, cur, covs, devs, gains, terms, links, work, sums, post, local_w,
        state_sem, weight_sem, push, here) = scratch[3 * batches:]
    h, lev = lax.axis_index("horiz"), lax.axis_index("lev")
    x, z, core = h // (2 * Z_DIM), (h // 2) % Z_DIM, h % 2
    lanes = lax.broadcasted_iota(jnp.int32, (N, N), 1)
    eye = lanes == lax.broadcasted_iota(jnp.int32, (N, N), 0)
    member = lanes < M

    near_peers = [rank((x + s) % X_DIM, z, (core + c) % 2) for s in range(X_DIM) for c in range(2) if s or c]
    near_peers = [{"horiz": to, "lev": lev} for to in near_peers]
    line_peers = [{"horiz": rank(x, (z + s) % Z_DIM, core), "lev": lev} for s in range(1, Z_DIM)]
    level_peers = [{"horiz": h, "lev": (lev + s) % Y_DIM} for s in range(1, Y_DIM)]
    peers = [near_peers, line_peers, level_peers, [{"horiz": rank(x, z, 1 - core), "lev": lev}]]

    barrier = pltpu.get_barrier_semaphore()
    for to in near_peers + line_peers + level_peers:
        pl.semaphore_signal(barrier, inc=1, device_id=to, device_id_type=MESH)

    def slab(t, outward):
        inside, far = post.at[:, t * N:(t + 1) * N], (post_out if outward else state).at[:, t, :]
        return pltpu.make_async_copy(inside if outward else far, far if outward else inside, state_sem.at[t])
    fetch = pltpu.make_async_copy(weights, local_w, weight_sem)

    def shared(b):
        return b >= WHOLE_GROUPS

    def half(b, which):
        rows = PER_LEVEL // 2
        return pl.ds(pl.multiple_of(which * rows, rows), rows) if shared(b) else slice(None)

    def group(b):
        return slice(first(b), first(b + 1))

    def copies(b, stage):
        if stage == 0:
            source, target = send.at[group(b)], near[b].at[x * 2 + core]
        elif stage == 1:
            source, target = picked[b].at[:, half(b, core)], line[b].at[z]
        elif stage == 2:
            source, target = line[b].at[Z_DIM], mats.at[group(b), lev, half(b, core)]
        else:
            source = target = mats.at[group(b), :, half(b, core)]
        return [
            pltpu.make_async_remote_copy(source, target, push.at[b, stage, i], here.at[b, stage], device_id=to, device_id_type=MESH)
            for i, to in enumerate(peers[stage])
        ]

    def start(b, stage):
        owner = owner_ids[b]
        if stage == 0:
            near[b][x * 2 + core] = send[group(b)]
        elif stage == 1:
            picked[b][...] = near[b][(owner // (2 * Z_DIM)) * 2 + owner % 2]
            line[b][z] = picked[b][:, half(b, core)]
        elif stage == 2:
            block = line[b][(owner // 2) % Z_DIM]
            line[b][Z_DIM] = block
            mats[group(b), lev, half(b, core)] = block
        for copy in copies(b, stage):
            copy.start()

    def arrived(b, stage):
        count = len(peers[stage])
        if stage < 2:
            whole = [near, line][stage][b].at[0:count]
        else:
            whole = mats.at[group(b), 0:count, half(b, core)] if stage == 2 else mats.at[group(b), :, half(b, 1 - core)]
        pltpu.make_async_copy(whole, whole, here.at[b, stage]).wait()

    def advance(b, stage):
        if b < batches:
            if stage > 0:
                arrived(b, stage - 1)
            start(b, stage)

    def arrive(c):
        arrived(c, 3 if shared(c) else 2)
        cur[c] = centred(mats[first(c)].reshape(N, N))

    def weight(c, a):
        return mats[first(c) + 1 + a].reshape(N, N)

    def column(row):
        return jnp.sum(jnp.where(eye, row, 0.0), axis=1, keepdims=True)

    def centred(priors):
        mean = jnp.sum(jnp.where(member, priors, 0.0), axis=1, keepdims=True) / M
        return jnp.where(member, priors - mean, jnp.where(lanes == M, mean, 0.0))

    def link(c, a):
        return dot(cur[c], devs[a], 1, 1) * weight(c, a) * (1.0 / (M - 1.0))

    def carry_over(c, a):
        cur[c] = cur[c] + dot(link(c, a), gains[a])

    def whole(split):
        return split + jnp.sum(jnp.where(lanes == M, split, 0.0), axis=1, keepdims=True)

    def halves(x):
        h = x.astype(bf16)
        return h, (x - h.astype(f32)).astype(bf16)

    def finish(b):
        held = {}

        def prepare():
            incs[b] = dot(whole(terms[b]), covs[b], 0, 1)[:M]
            dh, dl = halves(devs[b][:, :M])
            held["d"] = jnp.concatenate([dh, dl, dh], axis=1)
            gh, gl = halves(whole(gains[b]).T[:M] * (1.0 / (M - 1.0)))
            held["g"] = jnp.concatenate([gh, gl, gh], axis=1)
            held["w"] = local_w[b].T
        wide = tiles * BLOCK

        def part(index):
            cs = wide * index
            old = post[:, cs:cs + wide]
            xh, xl = halves(old)
            r = dot(held["d"], jnp.concatenate([xh, xh, xl], axis=0), precision=None)
            scale = [jnp.broadcast_to(held["w"][:, t:t + 1], (N, N)) for t in range(cs // N, (cs + wide) // N)]
            rh, rl = halves(r * jnp.concatenate(scale, axis=1))
            post[:, cs:cs + wide] = old + dot(held["g"], jnp.concatenate([rh, rh, rl], axis=0), precision=None)
        return [prepare] + [lambda index=index: part(index) for index in range(tiles * N // wide)]

    def batch(b, services):
        blocks = N // BLOCK
        share = [[] for _ in range(blocks)]
        if b > 0:
            for k, step in enumerate(finish(b - 1)):
                share[max(k - 1, 0)].append(step)
        if b + 1 < batches:
            at = ARRIVAL[b]
            share[at].append(lambda: arrive(b + 1))
            for a in range(b):
                share[min(at + a, blocks - 1)].append(lambda a=a: carry_over(b + 1, a))

            def last_link():
                links[b] = link(b + 1, b)
            share[min(at + b, blocks - 1)].append(last_link)

        def beside(block):
            for group_moved, stage in services.get(block, ()):
                advance(group_moved, stage)
            for step in share[block]:
                step()
        p = cur[b]
        devs[b] = jnp.where(member, p, 0.0)
        dev = devs[b]
        var_row = variance[b:b + 1, :]
        var_col = column(var_row)
        cov = dot(dev, dev, 1, 1) * (1.0 / (M - 1.0))
        covs[b] = cov
        work[:, 0:N] = jnp.where(eye, cov + var_row, cov)
        work[:, N:2 * N] = jnp.where(lanes == M, column(observed[b:b + 1, :]) - p, dev)
        eliminate(work, sums, jnp.sqrt(var_col), beside)
        t = sums[:, N:2 * N]
        terms[b] = t
        gain = t - dot(sums[:, 0:N], var_col * t)
        gains[b] = gain
        if b + 1 < batches:
            cur[b + 1] = cur[b + 1] + dot(links[b], gain)

    pl.semaphore_wait(barrier, len(near_peers) + len(line_peers) + len(level_peers))
    advance(0, 0)
    advance(1, 0)
    advance(2, 0)
    for t in range(tiles):
        slab(t, False).start()
    fetch.start()
    advance(0, 1)
    advance(1, 1)
    advance(3, 0)
    advance(0, 2)
    advance(2, 1)
    advance(1, 2)
    advance(4, 0)
    arrive(0)
    services = SERVICES
    for b in range(batches):
        if b == 1:
            for t in range(tiles):
                slab(t, False).wait()
            fetch.wait()
        batch(b, services.get(b, {}))
    for step in finish(batches - 1):
        step()

    for t in range(tiles):
        slab(t, True).start()
    for b in range(batches):
        for stage in range(4 if shared(b) else 3):
            for copy in copies(b, stage):
                copy.wait_send()
    for t in range(tiles):
        slab(t, True).wait()


def extract_kernel(obs_cell, state, weights, send):
    batches, tiles = weights.shape[0], weights.shape[1]
    lev = lax.axis_index("lev")
    lane = lax.broadcasted_iota(jnp.int32, (M, N), 1)
    for b in range(batches):
        gathered = jnp.zeros((M, N), f32)
        for j in range(PER_LEVEL):
            cell = obs_cell[b, lev * PER_LEVEL + j]
            tile, at = cell // TILE, cell % TILE
            chunk = state[pl.ds(tile, M, stride=tiles), :]
            gathered = jnp.where(lane == j, pltpu.roll(chunk, lax.rem(j - at + N, N), 1), gathered)
            for a in range(b):
                send[first(b) + 1 + a, j:j + 1, :] = weights[a, pl.ds(tile, 1), :]
        square = jnp.concatenate([gathered, jnp.zeros((N - M, N), f32)], axis=0)
        send[first(b)] = square.T[:PER_LEVEL]


def extract(obs_cell, state, weights):
    vm = pl.BlockSpec(memory_space=pltpu.VMEM)
    return pl.pallas_call(
        extract_kernel,
        out_shape=jax.ShapeDtypeStruct((first(obs_cell.shape[0]), PER_LEVEL, N), f32),
        in_specs=[pl.BlockSpec(memory_space=pltpu.SMEM), vm, vm],
        out_specs=vm,
        compiler_params=pltpu.CompilerParams(vmem_limit_bytes=48 << 20),
    )(obs_cell, state, weights)


def assimilate(owner_ids, send, observed, variance, state, weights):
    batches = observed.shape[0]
    tiles = state.shape[1]
    vm = pl.BlockSpec(memory_space=pltpu.VMEM)
    smem = pl.BlockSpec(memory_space=pltpu.SMEM)
    hbm = pl.BlockSpec(memory_space=pl.ANY)
    dma = pltpu.SemaphoreType.DMA

    def block(*lead):
        return pltpu.VMEM((*lead, N), f32)
    groups = [(b + 1, PER_LEVEL) for b in range(batches)]
    parts = [(b + 1, PER_LEVEL // (1 if b < WHOLE_GROUPS else 2)) for b in range(batches)]
    return pl.pallas_call(
        kernel,
        out_shape=(jax.ShapeDtypeStruct(state.shape, f32), jax.ShapeDtypeStruct((batches, M, N), f32)),
        in_specs=[smem, vm, vm, vm, hbm, hbm],
        out_specs=(hbm, vm),
        scratch_shapes=[block(2 * X_DIM, *g) for g in groups] + [block(Z_DIM + 1, *g) for g in parts] + [block(*g) for g in groups] + [
            block(first(batches), Y_DIM, PER_LEVEL)] + [block(batches, N)] * 6 + [
            pltpu.VMEM((N, 2 * N), f32), pltpu.VMEM((N, 2 * N), f32), pltpu.VMEM((M, tiles * N), f32), block(batches, tiles),
            dma((tiles,)), dma, dma((batches, 4, max(2 * X_DIM, Z_DIM, Y_DIM) - 1)), dma((batches, 4)),
        ],
        compiler_params=pltpu.CompilerParams(vmem_limit_bytes=48 << 20, collective_id=0, has_side_effects=True),
        cost_estimate=pl.CostEstimate(flops=10**9, bytes_accessed=4 * 10**6, transcendentals=0),
    )(owner_ids, send, observed, variance, state, weights)


def local(prior_state, localization, observed, error_variance, owner_ids, obs_cell):
    members, _, cells = prior_state.shape
    tiles = cells // TILE
    batches = obs_cell.shape[0]
    weights = jnp.transpose(localization.reshape(batches, N, tiles), (0, 2, 1))
    send = extract(obs_cell, prior_state.reshape(members * tiles, TILE), weights)
    state, increments = assimilate(owner_ids, send, observed, error_variance, prior_state.reshape(members, tiles, TILE), weights)
    return state.reshape(members, 1, cells), jnp.transpose(increments, (0, 2, 1))


def solution(mesh):
    in_specs = (P(None, "lev", "horiz"), P(None, None, "lev", "horiz"), P(), P(), P(), P())
    out_specs = (P(None, "lev", "horiz"), P())
    return jax.shard_map(local, mesh=mesh, in_specs=in_specs, out_specs=out_specs, check_vma=False)
```

time: 99.6 us -> 84.1 us (0.84)
  the two profiles are of different devices: /device:TPU:2 before, /device:TPU:6 now
where the time goes in v3:
time: 84.1 us; the launch traced here: 83.9 us
  Pallas kernels  78.6 us (93%)
  local copies, waits for them, and re-layouts  4.67 us (6%)
    pallas_call x1, Pallas kernels, assimilate(): pl.pallas_call(kernel, out_shape=(jax.ShapeDtypeStruct(state.shape, f32),...  73.5 us
    pallas_call x1, Pallas kernels, extract(): pl.pallas_call(extract_kernel, out_shape=jax.ShapeDtypeStruct((first(obs_...  5.05 us
    unnamed x16, local copies, waits for them, and re-layouts  4.67 us

profile of v3, /device:TPU:6, one launch (start us, length us, event | category | flops | bytes accessed | tf_op | source)
XLA Modules:
  0.0 83.9 jit_solution(15989574142466028971)
XLA Ops:
  0.6 0.0 copy-start.6
  0.6 0.0 copy-start.4
  0.7 0.0 copy-start
  0.7 1.3 %copy-done = f32[80,1,4096]{2,1,0:T(1,128)S(1)} copy-done((f32[80,1,4096]{2,1,0:T(1,128)S(1)}, f32[80,1,4096]{2,1,0:T(1,128)}, u32[]{:S(2)}) %copy-start) | copy-done | bytes 1310744
  2.0 0.0 copy-start.2
  2.0 0.9 %copy-done.2 = f32[6,128,1,32]{1,3,2,0:T(8,128)S(1)} copy-done((f32[6,128,1,32]{1,3,2,0:T(8,128)S(1)}, f32[6,128,1,32]{1,3,2,0:T(8,128)}, u32[]{:S(2)}) %copy-start.2) | copy-done | bytes 98328
  2.9 0.0 copy-start.3
  2.9 0.7 copy-done.3
  3.6 0.0 copy-start.1
  3.6 0.0 copy-start.5
  3.6 5.0 %shard_map.77.send = f32[21,16,128]{2,1,0:T(8,128)S(1)} custom-call(s32[6,128]{1,0:T(8,128)S(1)} %copy-done.3, f32[2560,128]{1,0:T(8,128)S(1)} %bitcast.7, f32[6,32,128]{2,1,0:T(8,128)S(1)} %bitcast.11), custom_call_target="tpu_custom_call" | custom-call | tf_op jit(solution)/shard_map/pallas_call | solution.py:362
  8.6 0.0 copy-done.6
  8.6 0.0 copy-done.4
  8.6 0.0 copy-done.1
  8.6 0.0 copy-done.5
  8.6 73.5 %shard_map.78 = (f32[80,32,128]{2,1,0:T(8,128)S(1)}, f32[6,80,128]{2,1,0:T(8,128)S(1)}) custom-call(s32[6]{0:T(128)S(1)} %copy-done.6, f32[21,16,128]{2,1,0:T(8,128)S(1)} %shard_map.77.send, f32[6,128]{1,0:T(8,128)S(1)} %copy-done.4, f32[6,128]{1,0:T(8,128)S(1)} %copy-done.5, f32[80,32,128]{2,1,0:T(8,128)S(1)} %bitcast.8, f32[6,32,128]{2,1,0:T(8,128)S(1)} %bitcast.12), custom_call_target="tpu_custom_call" | custom-call | flops 1000000000 | bytes 4000000 | tf_op jit(solution)/shard_map/pallas_call | solution.py:383
  82.2 1.1 %copy.11 = f32[80,1,4096]{2,1,0:T(1,128)} copy(f32[80,1,4096]{2,1,0:T(1,128)S(1)} %bitcast.9) | data formatting | bytes 2621440
  83.2 0.7 copy.12
Async XLA Ops:
  0.6 8.0 %copy-start.6 = (s32[6]{0:T(128)S(1)}, s32[6]{0:T(128)}, u32[]{:S(2)}) copy-start(s32[6]{0:T(128)} %owner_ids.1) | copy-start | bytes 76
  0.6 8.0 %copy-start.4 = (f32[6,128]{1,0:T(8,128)S(1)}, f32[6,128]{1,0:T(8,128)}, u32[]{:S(2)}) copy-start(f32[6,128]{1,0:T(8,128)} %observed.1) | copy-start | bytes 9220
  0.7 1.3 %copy-start = (f32[80,1,4096]{2,1,0:T(1,128)S(1)}, f32[80,1,4096]{2,1,0:T(1,128)}, u32[]{:S(2)}) copy-start(f32[80,1,4096]{2,1,0:T(1,128)} %param.6) | copy-start | bytes 3932164
  2.0 0.9 %copy-start.2 = (f32[6,128,1,32]{1,3,2,0:T(8,128)S(1)}, f32[6,128,1,32]{1,3,2,0:T(8,128)}, u32[]{:S(2)}) copy-start(f32[6,128,1,32]{1,3,2,0:T(8,128)} %param.7) | copy-start | bytes 294916
  2.9 0.7 copy-start.3
  3.6 5.1 %copy-start.1 = (f32[80,1,4096]{2,1,0:T(1,128)S(1)}, f32[80,1,4096]{2,1,0:T(1,128)}, u32[]{:S(2)}) copy-start(f32[80,1,4096]{2,1,0:T(1,128)} %param.6) | copy-start | bytes 3932164
  3.6 5.1 %copy-start.5 = (f32[6,128]{1,0:T(8,128)S(1)}, f32[6,128]{1,0:T(8,128)}, u32[]{:S(2)}) copy-start(f32[6,128]{1,0:T(8,128)} %variance.1) | copy-start | bytes 9220

commit v4 on v3

--- a/solution.py
+++ b/solution.py
@@ -14,6 +14,7 @@
 N, M = 128, 80
 PER_LEVEL = N // Y_DIM
 WHOLE_GROUPS = 2
+PLACES = (0, 0, 1, 2, 3, 4, 6, 8, 9)
 ARRIVAL = (7, 5, 3, 3, 3)
 SERVICES = {
     0: {0: [(3, 1)], 4: [(2, 2), (5, 0), (4, 1)]},
@@ -43,6 +44,8 @@
 
 
 BLOCK = 16
+AHEAD = 16
+SUMMED = 32
 
 
 def lane_copy(tile, lane):
@@ -57,8 +60,9 @@
     row8 = lax.broadcasted_iota(jnp.int32, (8, N), 0)
     lane8 = lax.broadcasted_iota(jnp.int32, (8, N), 1)
     own = BLOCK // 8
+    kept_a, kept_m = [], []
     for r0 in range(0, N, BLOCK):
-        tall = min(2 * BLOCK, N - r0) // 8
+        tall = min(BLOCK + AHEAD, N - r0) // 8
         inside = (lane8 >= r0) & (lane8 < r0 + BLOCK)
         win_s = [work[r0 + 8 * t:r0 + 8 * t + 8, 0:N] for t in range(tall)]
         win_d = [work[r0 + 8 * t:r0 + 8 * t + 8, N:2 * N] for t in range(tall)]
@@ -110,7 +114,7 @@
             work[r0 + 8 * t:r0 + 8 * t + 8, 0:N] = win_s[t]
             work[r0 + 8 * t:r0 + 8 * t + 8, N:2 * N] = win_d[t]
         block_s = jnp.concatenate(win_s[:own], axis=0)
-        low = r0 + 2 * BLOCK
+        low = r0 + BLOCK + AHEAD
         if low < N:
             left = jnp.concatenate([win_s[t] / diag[t] for t in range(own)], axis=0)
             right = jnp.concatenate([block_s, jnp.concatenate([win_d[t] * shrink[t] for t in range(own)], axis=0)], axis=1)
@@ -119,13 +123,17 @@
             gone = lax.broadcasted_iota(jnp.int32, old.shape, 1)
             work[low:, 0:N] = jnp.where((gone >= r0) & (gone < r0 + BLOCK), 0.0, old) - update[low:, 0:N]
             work[low:, N:2 * N] = work[low:, N:2 * N] - update[low:, N:2 * N]
-        a = jnp.concatenate([jnp.where(lane8 < r0 + BLOCK, win_s[t] * inv[t], 0.0) for t in range(own)], axis=0)
-        m = jnp.concatenate([win_d[t] * jnp.where(lane8 < M, -1.0 / (f[t] + roots[t]), inv[t]) for t in range(own)], axis=0)
-        update = panel_product(a, jnp.concatenate([a, m], axis=1))
-        if r0 == 0:
-            sums[...] = update
-        else:
-            sums[0:r0 + BLOCK, :] = sums[0:r0 + BLOCK, :] + update[0:r0 + BLOCK]
+        kept_a += [jnp.where(lane8 < r0 + BLOCK, win_s[t] * inv[t], 0.0) for t in range(own)]
+        kept_m += [win_d[t] * jnp.where(lane8 < M, -1.0 / (f[t] + roots[t]), inv[t]) for t in range(own)]
+        if len(kept_a) == SUMMED // 8:
+            a, m = jnp.concatenate(kept_a, axis=0), jnp.concatenate(kept_m, axis=0)
+            kept_a, kept_m = [], []
+            update = panel_product(a, jnp.concatenate([a, m], axis=1))
+            done = r0 + BLOCK
+            if done == SUMMED:
+                sums[...] = update
+            else:
+                sums[0:done, :] = sums[0:done, :] + update[0:done]
         beside(r0 // BLOCK)
 
 
@@ -137,13 +145,47 @@
     return (x * Z_DIM + z) * 2 + core
 
 
-def kernel(owner_ids, send, observed, variance, state, weights, post_out, incs, *scratch):
+def halves(x):
+    h = x.astype(bf16)
+    return h, (x - h.astype(f32)).astype(bf16)
+
+
+def whole(split):
+    lanes = lax.broadcasted_iota(jnp.int32, split.shape, 1)
+    return split + jnp.sum(jnp.where(lanes == M, split, 0.0), axis=1, keepdims=True)
+
+
+def finish(dev, gain, term, cov, weights, old, new, increments):
+    cells = old.shape[1]
+    held = {}
+
+    def prepare():
+        increments(dot(whole(term()), cov(), 0, 1)[:M])
+        dh, dl = halves(dev()[:, :M])
+        held["d"] = jnp.concatenate([dh, dl, dh], axis=1)
+        gh, gl = halves(whole(gain()).T[:M] * (1.0 / (M - 1.0)))
+        held["g"] = jnp.concatenate([gh, gl, gh], axis=1)
+        held["w"] = weights().T
+    wide = 4 * N
+
+    def part(index):
+        cs = wide * index
+        x = old[:, cs:cs + wide]
+        xh, xl = halves(x)
+        r = dot(held["d"], jnp.concatenate([xh, xh, xl], axis=0), precision=None)
+        scale = [jnp.broadcast_to(held["w"][:, t:t + 1], (N, N)) for t in range(cs // N, (cs + wide) // N)]
+        rh, rl = halves(r * jnp.concatenate(scale, axis=1))
+        new[:, cs:cs + wide] = x + dot(held["g"], jnp.concatenate([rh, rh, rl], axis=0), precision=None)
+    return [prepare] + [lambda index=index: part(index) for index in range(cells // wide)]
+
+
+def kernel(owner_ids, obs_cell, observed, variance, state, weights, post_out, incs, last, last_w, *scratch):
     batches = observed.shape[0]
     tiles = state.shape[1]
     near = scratch[0:batches]
     line = scratch[batches:2 * batches]
     picked = scratch[2 * batches:3 * batches]
-    (mats, cur, covs, devs, gains, terms, links, work, sums, post, local_w,
+    (send, mats, cur, covs, devs, gains, terms, links, work, sums, post, local_w,
         state_sem, weight_sem, push, here) = scratch[3 * batches:]
     h, lev = lax.axis_index("horiz"), lax.axis_index("lev")
     x, z, core = h // (2 * Z_DIM), (h // 2) % Z_DIM, h % 2
@@ -161,9 +203,11 @@
     for to in near_peers + line_peers + level_peers:
         pl.semaphore_signal(barrier, inc=1, device_id=to, device_id_type=MESH)
 
-    def slab(t, outward):
-        inside, far = post.at[:, t * N:(t + 1) * N], (post_out if outward else state).at[:, t, :]
-        return pltpu.make_async_copy(inside if outward else far, far if outward else inside, state_sem.at[t])
+    def slab(t):
+        return pltpu.make_async_copy(state.at[:, t, :], post.at[:, t * N:(t + 1) * N], state_sem.at[t])
+    def onward(k):
+        chunk = slice(4 * N * k, 4 * N * (k + 1))
+        return pltpu.make_async_copy(post.at[:, chunk], post_out.at[:, chunk], state_sem.at[k])
     fetch = pltpu.make_async_copy(weights, local_w, weight_sem)
 
     def shared(b):
@@ -238,41 +282,17 @@
     def carry_over(c, a):
         cur[c] = cur[c] + dot(link(c, a), gains[a])
 
-    def whole(split):
-        return split + jnp.sum(jnp.where(lanes == M, split, 0.0), axis=1, keepdims=True)
-
-    def halves(x):
-        h = x.astype(bf16)
-        return h, (x - h.astype(f32)).astype(bf16)
-
-    def finish(b):
-        held = {}
-
-        def prepare():
-            incs[b] = dot(whole(terms[b]), covs[b], 0, 1)[:M]
-            dh, dl = halves(devs[b][:, :M])
-            held["d"] = jnp.concatenate([dh, dl, dh], axis=1)
-            gh, gl = halves(whole(gains[b]).T[:M] * (1.0 / (M - 1.0)))
-            held["g"] = jnp.concatenate([gh, gl, gh], axis=1)
-            held["w"] = local_w[b].T
-        wide = tiles * BLOCK
-
-        def part(index):
-            cs = wide * index
-            old = post[:, cs:cs + wide]
-            xh, xl = halves(old)
-            r = dot(held["d"], jnp.concatenate([xh, xh, xl], axis=0), precision=None)
-            scale = [jnp.broadcast_to(held["w"][:, t:t + 1], (N, N)) for t in range(cs // N, (cs + wide) // N)]
-            rh, rl = halves(r * jnp.concatenate(scale, axis=1))
-            post[:, cs:cs + wide] = old + dot(held["g"], jnp.concatenate([rh, rh, rl], axis=0), precision=None)
-        return [prepare] + [lambda index=index: part(index) for index in range(tiles * N // wide)]
-
     def batch(b, services):
         blocks = N // BLOCK
-        share = [[] for _ in range(blocks)]
+        share = [[] for _ in range(blocks + 2)]
         if b > 0:
-            for k, step in enumerate(finish(b - 1)):
-                share[max(k - 1, 0)].append(step)
+            def keep(value):
+                incs[b - 1] = value
+            before = finish(*[lambda ref=ref: ref[b - 1] for ref in (devs, gains, terms, covs, local_w)], post, post, keep)
+            for k, step in enumerate(before):
+                if b == batches - 1 and k > 0:
+                    step = lambda k=k, step=step: (step(), onward(k - 1).start())
+                share[PLACES[k]].append(step)
         if b + 1 < batches:
             at = ARRIVAL[b]
             share[at].append(lambda: arrive(b + 1))
@@ -300,18 +320,45 @@
         eliminate(work, sums, jnp.sqrt(var_col), beside)
         t = sums[:, N:2 * N]
         terms[b] = t
+        beside(blocks)
         gain = t - dot(sums[:, 0:N], var_col * t)
         gains[b] = gain
+        beside(blocks + 1)
         if b + 1 < batches:
             cur[b + 1] = cur[b + 1] + dot(links[b], gain)
 
+    for t in range(tiles):
+        slab(t).start()
+    fetch.start()
+    row_lanes = lax.broadcasted_iota(jnp.int32, (8, N), 1)
+    cells = jnp.zeros((8, N), jnp.int32)
+    for b in range(batches):
+        turned = pltpu.roll(jnp.broadcast_to(obs_cell[b:b + 1, :], (8, N)), (b * PER_LEVEL - lev * PER_LEVEL + N) % N, 1)
+        cells = jnp.where((row_lanes >= b * PER_LEVEL) & (row_lanes < (b + 1) * PER_LEVEL), turned, cells)
+    cells = cells[0:1]
+    tile_of = column((cells // TILE).astype(f32))
+    in_tile = jnp.where(lax.broadcasted_iota(jnp.int32, (N, tiles), 1).astype(f32) == tile_of, 1.0, 0.0)
+    wide = 4 * N
+    gathered = jnp.zeros((3 * M, N), f32)
+    for cs in range(0, tiles * N, wide):
+        for t in range(cs // N, (cs + wide) // N):
+            slab(t).wait()
+        parts = jnp.concatenate(split3(post[:, cs:cs + wide]), axis=0).astype(bf16)
+        chosen = jnp.where(lax.broadcasted_iota(jnp.int32, (wide, N), 0) + cs == cells, 1.0, 0.0).astype(bf16)
+        gathered = gathered + dot(parts, chosen, precision=None)
+    gathered = gathered[:M] + gathered[M:2 * M] + gathered[2 * M:]
+    rows = jnp.concatenate([gathered, jnp.zeros((N - M, N), f32)], axis=0).T
+    for b in range(batches):
+        send[first(b)] = rows[b * PER_LEVEL:(b + 1) * PER_LEVEL]
     pl.semaphore_wait(barrier, len(near_peers) + len(line_peers) + len(level_peers))
     advance(0, 0)
+    fetch.wait()
+    for a in range(batches - 1):
+        rows = dot(in_tile, local_w[a])
+        for b in range(a + 1, batches):
+            send[first(b) + 1 + a] = rows[b * PER_LEVEL:(b + 1) * PER_LEVEL]
     advance(1, 0)
     advance(2, 0)
-    for t in range(tiles):
-        slab(t, False).start()
-    fetch.start()
     advance(0, 1)
     advance(1, 1)
     advance(3, 0)
@@ -322,58 +369,78 @@
     arrive(0)
     services = SERVICES
     for b in range(batches):
-        if b == 1:
-            for t in range(tiles):
-                slab(t, False).wait()
-            fetch.wait()
         batch(b, services.get(b, {}))
-    for step in finish(batches - 1):
-        step()
-
-    for t in range(tiles):
-        slab(t, True).start()
+    for k, ref in enumerate((devs, gains, terms, covs)):
+        last[k] = ref[batches - 1]
+    last_w[...] = local_w[batches - 1]
+    for k in range(tiles // 4):
+        onward(k).wait()
     for b in range(batches):
         for stage in range(4 if shared(b) else 3):
             for copy in copies(b, stage):
                 copy.wait_send()
+
+
+def last_kernel(slab, incs, factors, weights, state_out, incs_out, old, new, held, held_w, last_inc, state_sem, slab_sem, small_sem):
+    batches = incs.shape[0]
+    tiles = state_out.shape[1]
+
+    def inward(k):
+        chunk = slice(4 * N * k, 4 * N * (k + 1))
+        return pltpu.make_async_copy(slab.at[:, chunk], old.at[:, chunk], slab_sem.at[k])
+
+    def outward(t):
+        return pltpu.make_async_copy(new.at[:, t * N:(t + 1) * N], state_out.at[:, t, :], state_sem.at[t])
+    small = [
+        pltpu.make_async_copy(factors, held, small_sem.at[0]),
+        pltpu.make_async_copy(weights, held_w, small_sem.at[1]),
+        pltpu.make_async_copy(incs.at[0:batches - 1], incs_out.at[0:batches - 1], small_sem.at[2]),
+    ]
+    own = pltpu.make_async_copy(last_inc, incs_out.at[batches - 1], small_sem.at[3])
+    for copy in small[:2] + [inward(k) for k in range(tiles // 4)] + small[2:]:
+        copy.start()
+
+    def keep(value):
+        last_inc[...] = value
+    steps = finish(*[lambda k=k: held[k] for k in range(4)], lambda: held_w[...], old, new, keep)
+    for copy in small[:2]:
+        copy.wait()
+    for k, step in enumerate(steps):
+        if k == 0:
+            step()
+            own.start()
+        else:
+            inward(k - 1).wait()
+            step()
+            for t in range(4 * (k - 1), 4 * k):
+                outward(t).start()
+    small[2].wait()
+    own.wait()
     for t in range(tiles):
-        slab(t, True).wait()
-
-
-def extract_kernel(obs_cell, state, weights, send):
-    batches, tiles = weights.shape[0], weights.shape[1]
-    lev = lax.axis_index("lev")
-    lane = lax.broadcasted_iota(jnp.int32, (M, N), 1)
-    for b in range(batches):
-        gathered = jnp.zeros((M, N), f32)
-        for j in range(PER_LEVEL):
-            cell = obs_cell[b, lev * PER_LEVEL + j]
-            tile, at = cell // TILE, cell % TILE
-            chunk = state[pl.ds(tile, M, stride=tiles), :]
-            gathered = jnp.where(lane == j, pltpu.roll(chunk, lax.rem(j - at + N, N), 1), gathered)
-            for a in range(b):
-                send[first(b) + 1 + a, j:j + 1, :] = weights[a, pl.ds(tile, 1), :]
-        square = jnp.concatenate([gathered, jnp.zeros((N - M, N), f32)], axis=0)
-        send[first(b)] = square.T[:PER_LEVEL]
-
-
-def extract(obs_cell, state, weights):
-    vm = pl.BlockSpec(memory_space=pltpu.VMEM)
+        outward(t).wait()
+
+
+def conclude(slab, incs, factors, weights, state_shape):
+    hbm = pl.BlockSpec(memory_space=pltpu.MemorySpace.HBM)
+    dma = pltpu.SemaphoreType.DMA
     return pl.pallas_call(
-        extract_kernel,
-        out_shape=jax.ShapeDtypeStruct((first(obs_cell.shape[0]), PER_LEVEL, N), f32),
-        in_specs=[pl.BlockSpec(memory_space=pltpu.SMEM), vm, vm],
-        out_specs=vm,
-        compiler_params=pltpu.CompilerParams(vmem_limit_bytes=48 << 20),
-    )(obs_cell, state, weights)
-
-
-def assimilate(owner_ids, send, observed, variance, state, weights):
+        last_kernel,
+        out_shape=(jax.ShapeDtypeStruct(state_shape, f32), jax.ShapeDtypeStruct(incs.shape, f32)),
+        in_specs=[hbm] * 4,
+        out_specs=(hbm, hbm),
+        scratch_shapes=[pltpu.VMEM(ref.shape, f32) for ref in (slab, slab, factors, weights)] + [
+            pltpu.VMEM((M, N), f32), dma((state_shape[1],)), dma((state_shape[1] // 4,)), dma((4,)),
+        ],
+        compiler_params=pltpu.CompilerParams(vmem_limit_bytes=60 << 20),
+    )(slab, incs, factors, weights)
+
+
+def assimilate(owner_ids, obs_cell, observed, variance, state, weights):
     batches = observed.shape[0]
     tiles = state.shape[1]
     vm = pl.BlockSpec(memory_space=pltpu.VMEM)
     smem = pl.BlockSpec(memory_space=pltpu.SMEM)
-    hbm = pl.BlockSpec(memory_space=pl.ANY)
+    hbm = pl.BlockSpec(memory_space=pltpu.MemorySpace.HBM)
     dma = pltpu.SemaphoreType.DMA
 
     def block(*lead):
@@ -382,17 +449,18 @@
     parts = [(b + 1, PER_LEVEL // (1 if b < WHOLE_GROUPS else 2)) for b in range(batches)]
     return pl.pallas_call(
         kernel,
-        out_shape=(jax.ShapeDtypeStruct(state.shape, f32), jax.ShapeDtypeStruct((batches, M, N), f32)),
+        out_shape=tuple(jax.ShapeDtypeStruct(shape, f32) for shape in (
+            (M, tiles * N), (batches, M, N), (4, N, N), (tiles, N))),
         in_specs=[smem, vm, vm, vm, hbm, hbm],
-        out_specs=(hbm, vm),
+        out_specs=(hbm, vm, vm, vm),
         scratch_shapes=[block(2 * X_DIM, *g) for g in groups] + [block(Z_DIM + 1, *g) for g in parts] + [block(*g) for g in groups] + [
-            block(first(batches), Y_DIM, PER_LEVEL)] + [block(batches, N)] * 6 + [
+            block(first(batches), PER_LEVEL), block(first(batches), Y_DIM, PER_LEVEL)] + [block(batches, N)] * 6 + [
             pltpu.VMEM((N, 2 * N), f32), pltpu.VMEM((N, 2 * N), f32), pltpu.VMEM((M, tiles * N), f32), block(batches, tiles),
             dma((tiles,)), dma, dma((batches, 4, max(2 * X_DIM, Z_DIM, Y_DIM) - 1)), dma((batches, 4)),
         ],
-        compiler_params=pltpu.CompilerParams(vmem_limit_bytes=48 << 20, collective_id=0, has_side_effects=True),
+        compiler_params=pltpu.CompilerParams(vmem_limit_bytes=60 << 20, collective_id=0, has_side_effects=True),
         cost_estimate=pl.CostEstimate(flops=10**9, bytes_accessed=4 * 10**6, transcendentals=0),
-    )(owner_ids, send, observed, variance, state, weights)
+    )(owner_ids, obs_cell, observed, variance, state, weights)
 
 
 def local(prior_state, localization, observed, error_variance, owner_ids, obs_cell):
@@ -400,8 +468,9 @@
     tiles = cells // TILE
     batches = obs_cell.shape[0]
     weights = jnp.transpose(localization.reshape(batches, N, tiles), (0, 2, 1))
-    send = extract(obs_cell, prior_state.reshape(members * tiles, TILE), weights)
-    state, increments = assimilate(owner_ids, send, observed, error_variance, prior_state.reshape(members, tiles, TILE), weights)
+    state = prior_state.reshape(members, tiles, TILE)
+    slab, increments, factors, last_weights = assimilate(owner_ids, obs_cell, observed, error_variance, state, weights)
+    state, increments = conclude(slab, increments, factors, last_weights, state.shape)
     return state.reshape(members, 1, cells), jnp.transpose(increments, (0, 2, 1))
 
 

time: 84.1 us -> 78.3 us (0.931)
  the two profiles are of different devices: /device:TPU:6 before, /device:TPU:1 now
where the time goes in v4:
time: 78.3 us; the launch traced here: 77.2 us
  Pallas kernels  76.4 us (98%)
  between operations  0.82 us (1%)
    pallas_call x1, Pallas kernels, assimilate(): pl.pallas_call(kernel, out_shape=tuple((jax.ShapeDtypeStruct(shape, f32)...  68.6 us
    pallas_call x1, Pallas kernels, conclude(): pl.pallas_call(last_kernel, out_shape=(jax.ShapeDtypeStruct(state_shape,...  7.76 us

profile of v4, /device:TPU:1, one launch (start us, length us, event | category | flops | bytes accessed | tf_op | source)
XLA Modules:
  0.0 77.2 jit_solution(1824197439001374502)
XLA Ops:
  0.6 68.6 %shard_map.77 = (f32[80,4096]{1,0:T(8,128)}, f32[6,80,128]{2,1,0:T(8,128)}, f32[4,128,128]{2,1,0:T(8,128)}, f32[32,128]{1,0:T(8,128)}) custom-call(s32[6]{0:T(128)} %owner_ids.1, s32[6,128]{1,0:T(8,128)} %obs_cell.1, f32[6,128]{1,0:T(8,128)} %observed.1, f32[6,128]{1,0:T(8,128)} %variance.1, f32[80,32,128]{2,1,0:T(8,128)} %bitcast.6, f32[6,32,128]{2,1,0:T(8,128)} %bitcast.9), custom_call_target="tpu_custom_call" | custom-call | flops 1000000000 | bytes 4000000 | tf_op jit(solution)/shard_map/pallas_call | solution.py:450
  69.2 7.8 %shard_map.78 = (f32[80,32,128]{2,1,0:T(8,128)}, f32[6,80,128]{2,1,0:T(8,128)}) custom-call(f32[80,4096]{1,0:T(8,128)} %get-tuple-element.8.slab, f32[6,80,128]{2,1,0:T(8,128)} %get-tuple-element.9.incs, f32[4,128,128]{2,1,0:T(8,128)} %get-tuple-element.10.factors, f32[32,128]{1,0:T(8,128)} %get-tuple-element.11.weights), custom_call_target="tpu_custom_call" | custom-call | tf_op jit(solution)/shard_map/pallas_call | solution.py:426

commit v5 on v4

--- a/solution.py
+++ b/solution.py
@@ -14,6 +14,7 @@
 N, M = 128, 80
 PER_LEVEL = N // Y_DIM
 WHOLE_GROUPS = 2
+GROUPED = 4
 PLACES = (0, 0, 1, 2, 3, 4, 6, 8, 9)
 ARRIVAL = (7, 5, 3, 3, 3)
 SERVICES = {
@@ -35,9 +36,9 @@
     return h, m, r - m
 
 
-def panel_product(left, right):
+def panel_product(left, right, rows):
     h, m, l = split3(left)
-    lhs = jnp.concatenate([h, h, m, m, h, l], axis=0).T.astype(bf16)
+    lhs = jnp.concatenate([h, h, m, m, h, l], axis=0).T[rows].astype(bf16)
     h, m, l = split3(right)
     rhs = jnp.concatenate([h, m, h, m, l, h], axis=0).astype(bf16)
     return lax.dot_general(lhs, rhs, (((1,), (0,)), ((), ())), preferred_element_type=f32)
@@ -45,7 +46,7 @@
 
 BLOCK = 16
 AHEAD = 16
-SUMMED = 32
+SUMMED = 16
 
 
 def lane_copy(tile, lane):
@@ -66,7 +67,7 @@
         inside = (lane8 >= r0) & (lane8 < r0 + BLOCK)
         win_s = [work[r0 + 8 * t:r0 + 8 * t + 8, 0:N] for t in range(tall)]
         win_d = [work[r0 + 8 * t:r0 + 8 * t + 8, N:2 * N] for t in range(tall)]
-        roots = [jnp.broadcast_to(root_col[r0 + 8 * t:r0 + 8 * t + 8, :], (8, N)) for t in range(own)]
+        roots = [root_col[r0 + 8 * t:r0 + 8 * t + 8, :] for t in range(own)]
         cols = [[lane_copy(w, r0 + k) for w in win_s] for k in range(BLOCK)]
         win_s = [jnp.where(inside, jnp.where(lane8 == row8 + (r0 + 8 * t), 1.0, 0.0) if t < own else 0.0, w) for t, w in enumerate(win_s)]
         diag = [jnp.ones((8, N), f32)] * own
@@ -118,22 +119,21 @@
         if low < N:
             left = jnp.concatenate([win_s[t] / diag[t] for t in range(own)], axis=0)
             right = jnp.concatenate([block_s, jnp.concatenate([win_d[t] * shrink[t] for t in range(own)], axis=0)], axis=1)
-            update = panel_product(left, right)
+            update = panel_product(left, right, slice(low, N))
             old = work[low:, 0:N]
             gone = lax.broadcasted_iota(jnp.int32, old.shape, 1)
-            work[low:, 0:N] = jnp.where((gone >= r0) & (gone < r0 + BLOCK), 0.0, old) - update[low:, 0:N]
-            work[low:, N:2 * N] = work[low:, N:2 * N] - update[low:, N:2 * N]
+            work[low:, 0:N] = jnp.where((gone >= r0) & (gone < r0 + BLOCK), 0.0, old) - update[:, 0:N]
+            work[low:, N:2 * N] = work[low:, N:2 * N] - update[:, N:2 * N]
         kept_a += [jnp.where(lane8 < r0 + BLOCK, win_s[t] * inv[t], 0.0) for t in range(own)]
         kept_m += [win_d[t] * jnp.where(lane8 < M, -1.0 / (f[t] + roots[t]), inv[t]) for t in range(own)]
         if len(kept_a) == SUMMED // 8:
             a, m = jnp.concatenate(kept_a, axis=0), jnp.concatenate(kept_m, axis=0)
             kept_a, kept_m = [], []
-            update = panel_product(a, jnp.concatenate([a, m], axis=1))
             done = r0 + BLOCK
-            if done == SUMMED:
-                sums[...] = update
-            else:
-                sums[0:done, :] = sums[0:done, :] + update[0:done]
+            update = panel_product(a, jnp.concatenate([a, m], axis=1), slice(0, done))
+            if done > SUMMED:
+                update = jnp.concatenate([sums[0:done - SUMMED, :] + update[0:done - SUMMED], update[done - SUMMED:]], axis=0)
+            sums[0:done, :] = update
         beside(r0 // BLOCK)
 
 
@@ -150,6 +150,19 @@
     return h, (x - h.astype(f32)).astype(bf16)
 
 
+def dot3(a, b, cb=0):
+    ah, al = halves(a)
+    bh, bl = halves(b)
+    return dot(jnp.concatenate([ah, al, ah], axis=1), jnp.concatenate([bh, bh, bl], axis=cb), 1, cb, precision=None)
+
+
+def dot6(a, b, cb=0):
+    ah, am, al = (x.astype(bf16) for x in split3(a))
+    bh, bm, bl = (x.astype(bf16) for x in split3(b))
+    left = jnp.concatenate([ah, ah, am, am, ah, al], axis=1)
+    return dot(left, jnp.concatenate([bh, bm, bh, bm, bl, bh], axis=cb), 1, cb, precision=None)
+
+
 def whole(split):
     lanes = lax.broadcasted_iota(jnp.int32, split.shape, 1)
     return split + jnp.sum(jnp.where(lanes == M, split, 0.0), axis=1, keepdims=True)
@@ -160,7 +173,7 @@
     held = {}
 
     def prepare():
-        increments(dot(whole(term()), cov(), 0, 1)[:M])
+        increments(dot6(whole(term()).T[:M], cov(), 1))
         dh, dl = halves(dev()[:, :M])
         held["d"] = jnp.concatenate([dh, dl, dh], axis=1)
         gh, gl = halves(whole(gain()).T[:M] * (1.0 / (M - 1.0)))
@@ -185,7 +198,7 @@
     near = scratch[0:batches]
     line = scratch[batches:2 * batches]
     picked = scratch[2 * batches:3 * batches]
-    (send, mats, cur, covs, devs, gains, terms, links, work, sums, post, local_w,
+    (send, mats, cur, covs, devs, gains, terms, links, sides, work, sums, post, local_w,
         state_sem, weight_sem, push, here) = scratch[3 * batches:]
     h, lev = lax.axis_index("horiz"), lax.axis_index("lev")
     x, z, core = h // (2 * Z_DIM), (h // 2) % Z_DIM, h % 2
@@ -272,15 +285,21 @@
     def column(row):
         return jnp.sum(jnp.where(eye, row, 0.0), axis=1, keepdims=True)
 
+    def take_sides(b):
+        var_col = column(variance[b:b + 1, :])
+        sides[b, 0] = jnp.broadcast_to(var_col, (N, N))
+        sides[b, 1] = jnp.broadcast_to(jnp.sqrt(var_col), (N, N))
+        sides[b, 2] = jnp.broadcast_to(column(observed[b:b + 1, :]), (N, N))
+
     def centred(priors):
         mean = jnp.sum(jnp.where(member, priors, 0.0), axis=1, keepdims=True) / M
         return jnp.where(member, priors - mean, jnp.where(lanes == M, mean, 0.0))
 
     def link(c, a):
-        return dot(cur[c], devs[a], 1, 1) * weight(c, a) * (1.0 / (M - 1.0))
+        return dot3(cur[c], devs[a], 1) * weight(c, a) * (1.0 / (M - 1.0))
 
     def carry_over(c, a):
-        cur[c] = cur[c] + dot(link(c, a), gains[a])
+        cur[c] = cur[c] + dot3(link(c, a), gains[a])
 
     def batch(b, services):
         blocks = N // BLOCK
@@ -312,20 +331,19 @@
         devs[b] = jnp.where(member, p, 0.0)
         dev = devs[b]
         var_row = variance[b:b + 1, :]
-        var_col = column(var_row)
-        cov = dot(dev, dev, 1, 1) * (1.0 / (M - 1.0))
+        cov = dot6(dev, dev, 1) * (1.0 / (M - 1.0))
         covs[b] = cov
         work[:, 0:N] = jnp.where(eye, cov + var_row, cov)
-        work[:, N:2 * N] = jnp.where(lanes == M, column(observed[b:b + 1, :]) - p, dev)
-        eliminate(work, sums, jnp.sqrt(var_col), beside)
+        work[:, N:2 * N] = jnp.where(lanes == M, sides[b, 2] - p, dev)
+        eliminate(work, sums, sides.at[b, 1], beside)
         t = sums[:, N:2 * N]
         terms[b] = t
         beside(blocks)
-        gain = t - dot(sums[:, 0:N], var_col * t)
+        gain = t - dot6(sums[:, 0:N], sides[b, 0] * t)
         gains[b] = gain
         beside(blocks + 1)
         if b + 1 < batches:
-            cur[b + 1] = cur[b + 1] + dot(links[b], gain)
+            cur[b + 1] = cur[b + 1] + dot3(links[b], gain)
 
     for t in range(tiles):
         slab(t).start()
@@ -359,6 +377,8 @@
             send[first(b) + 1 + a] = rows[b * PER_LEVEL:(b + 1) * PER_LEVEL]
     advance(1, 0)
     advance(2, 0)
+    for b in range(batches):
+        take_sides(b)
     advance(0, 1)
     advance(1, 1)
     advance(3, 0)
@@ -381,7 +401,7 @@
                 copy.wait_send()
 
 
-def last_kernel(slab, incs, factors, weights, state_out, incs_out, old, new, held, held_w, last_inc, state_sem, slab_sem, small_sem):
+def last_kernel(slab, incs, factors, weights, state_out, incs_out, old, new, held, held_w, held_incs, state_sem, slab_sem, small_sem):
     batches = incs.shape[0]
     tiles = state_out.shape[1]
 
@@ -394,28 +414,30 @@
     small = [
         pltpu.make_async_copy(factors, held, small_sem.at[0]),
         pltpu.make_async_copy(weights, held_w, small_sem.at[1]),
-        pltpu.make_async_copy(incs.at[0:batches - 1], incs_out.at[0:batches - 1], small_sem.at[2]),
+        pltpu.make_async_copy(incs.at[0:batches - 1], held_incs.at[0:batches - 1], small_sem.at[2]),
     ]
-    own = pltpu.make_async_copy(last_inc, incs_out.at[batches - 1], small_sem.at[3])
+    away = pltpu.make_async_copy(held_incs, incs_out, small_sem.at[3])
     for copy in small[:2] + [inward(k) for k in range(tiles // 4)] + small[2:]:
         copy.start()
 
     def keep(value):
-        last_inc[...] = value
+        held_incs[batches - 1] = value
     steps = finish(*[lambda k=k: held[k] for k in range(4)], lambda: held_w[...], old, new, keep)
     for copy in small[:2]:
         copy.wait()
     for k, step in enumerate(steps):
         if k == 0:
             step()
-            own.start()
+            small[2].wait()
+            away.start()
+            for part in range(tiles // 4):
+                inward(part).wait()
         else:
-            inward(k - 1).wait()
             step()
-            for t in range(4 * (k - 1), 4 * k):
+        if k > 0 and k % GROUPED == 0:
+            for t in range(4 * (k - GROUPED), 4 * k):
                 outward(t).start()
-    small[2].wait()
-    own.wait()
+    away.wait()
     for t in range(tiles):
         outward(t).wait()
 
@@ -429,7 +451,7 @@
         in_specs=[hbm] * 4,
         out_specs=(hbm, hbm),
         scratch_shapes=[pltpu.VMEM(ref.shape, f32) for ref in (slab, slab, factors, weights)] + [
-            pltpu.VMEM((M, N), f32), dma((state_shape[1],)), dma((state_shape[1] // 4,)), dma((4,)),
+            pltpu.VMEM(incs.shape, f32), dma((state_shape[1],)), dma((state_shape[1] // 4,)), dma((4,)),
         ],
         compiler_params=pltpu.CompilerParams(vmem_limit_bytes=60 << 20),
     )(slab, incs, factors, weights)
@@ -454,7 +476,7 @@
         in_specs=[smem, vm, vm, vm, hbm, hbm],
         out_specs=(hbm, vm, vm, vm),
         scratch_shapes=[block(2 * X_DIM, *g) for g in groups] + [block(Z_DIM + 1, *g) for g in parts] + [block(*g) for g in groups] + [
-            block(first(batches), PER_LEVEL), block(first(batches), Y_DIM, PER_LEVEL)] + [block(batches, N)] * 6 + [
+            block(first(batches), PER_LEVEL), block(first(batches), Y_DIM, PER_LEVEL)] + [block(batches, N)] * 6 + [block(batches, 3, N)] + [
             pltpu.VMEM((N, 2 * N), f32), pltpu.VMEM((N, 2 * N), f32), pltpu.VMEM((M, tiles * N), f32), block(batches, tiles),
             dma((tiles,)), dma, dma((batches, 4, max(2 * X_DIM, Z_DIM, Y_DIM) - 1)), dma((batches, 4)),
         ],

time: 78.3 us -> 74.3 us (0.949)
  Pallas kernels: 76.4 us -> 72.4 us
    pallas_call x1, Pallas kernels: 7.76 us -> 5.16 us  [conclude(): pl.pallas_call(last_kernel, out_shape=(jax.ShapeDtypeStruct(state_shape,...]
    pallas_call x1, Pallas kernels: 68.6 us -> 67.3 us  [assimilate(): pl.pallas_call(kernel, out_shape=tuple((jax.ShapeDtypeStruct(shape, f32)...]
where the time goes in v5:
time: 74.3 us; the launch traced here: 73.3 us
  Pallas kernels  72.4 us (97%)
  between operations  0.82 us (1%)
    pallas_call x1, Pallas kernels, assimilate(): pl.pallas_call(kernel, out_shape=tuple((jax.ShapeDtypeStruct(shape, f32)...  67.3 us
    pallas_call x1, Pallas kernels, conclude(): pl.pallas_call(last_kernel, out_shape=(jax.ShapeDtypeStruct(state_shape,...  5.16 us

profile of v5, /device:TPU:1, one launch (start us, length us, event | category | flops | bytes accessed | tf_op | source)
XLA Modules:
  0.0 73.3 jit_solution(1258552578780123270)
XLA Ops:
  0.6 67.3 %shard_map.77 = (f32[80,4096]{1,0:T(8,128)}, f32[6,80,128]{2,1,0:T(8,128)}, f32[4,128,128]{2,1,0:T(8,128)}, f32[32,128]{1,0:T(8,128)}) custom-call(s32[6]{0:T(128)} %owner_ids.1, s32[6,128]{1,0:T(8,128)} %obs_cell.1, f32[6,128]{1,0:T(8,128)} %observed.1, f32[6,128]{1,0:T(8,128)} %variance.1, f32[80,32,128]{2,1,0:T(8,128)} %bitcast.6, f32[6,32,128]{2,1,0:T(8,128)} %bitcast.9), custom_call_target="tpu_custom_call" | custom-call | flops 1000000000 | bytes 4000000 | tf_op jit(solution)/shard_map/pallas_call | solution.py:472
  67.9 5.2 %shard_map.78 = (f32[80,32,128]{2,1,0:T(8,128)}, f32[6,80,128]{2,1,0:T(8,128)}) custom-call(f32[80,4096]{1,0:T(8,128)} %get-tuple-element.8.slab, f32[6,80,128]{2,1,0:T(8,128)} %get-tuple-element.9.incs, f32[4,128,128]{2,1,0:T(8,128)} %get-tuple-element.10.factors, f32[32,128]{1,0:T(8,128)} %get-tuple-element.11.weights), custom_call_target="tpu_custom_call" | custom-call | tf_op jit(solution)/shard_map/pallas_call | solution.py:448

commit v6 on v5

--- a/solution.py
+++ b/solution.py
@@ -16,12 +16,13 @@
 WHOLE_GROUPS = 2
 GROUPED = 4
 PLACES = (0, 0, 1, 2, 3, 4, 6, 8, 9)
-ARRIVAL = (7, 5, 3, 3, 3)
+ARRIVAL = (7, 5, 3, 6, 4)
 SERVICES = {
-    0: {0: [(3, 1)], 4: [(2, 2), (5, 0), (4, 1)]},
-    1: {0: [(3, 2), (5, 1)], 3: [(2, 3)], 4: [(4, 2)], 7: [(3, 3)]},
-    2: {0: [(5, 2)], 4: [(4, 3)]},
-    3: {1: [(5, 3)]},
+    0: {2: [(4, 1), (5, 0)], 5: [(3, 2)], 6: [(5, 1)]},
+    1: {2: [(2, 3)], 7: [(4, 2)]},
+    2: {1: [(3, 3)], 4: [(5, 2)]},
+    3: {4: [(4, 3)]},
+    4: {2: [(5, 3)]},
 }
 
 
@@ -382,10 +383,12 @@
     advance(0, 1)
     advance(1, 1)
     advance(3, 0)
+    advance(2, 1)
     advance(0, 2)
-    advance(2, 1)
+    advance(4, 0)
     advance(1, 2)
-    advance(4, 0)
+    advance(3, 1)
+    advance(2, 2)
     arrive(0)
     services = SERVICES
     for b in range(batches):

time: 74.3 us -> 73.2 us (0.985); the launches traced: 73.3 us -> 73 us
  no operation moved by 1% of the time
where the time goes in v6:
time: 73.2 us; the launch traced here: 73 us
  Pallas kernels  72.2 us (99%)
  between operations  0.82 us (1%)
    pallas_call x1, Pallas kernels, assimilate(): pl.pallas_call(kernel, out_shape=tuple((jax.ShapeDtypeStruct(shape, f32)...  67 us
    pallas_call x1, Pallas kernels, conclude(): pl.pallas_call(last_kernel, out_shape=(jax.ShapeDtypeStruct(state_shape,...  5.16 us

profile of v6, /device:TPU:1, one launch (start us, length us, event | category | flops | bytes accessed | tf_op | source)
XLA Modules:
  0.0 73.0 jit_solution(10575781377949704364)
XLA Ops:
  0.6 67.0 %shard_map.77 = (f32[80,4096]{1,0:T(8,128)}, f32[6,80,128]{2,1,0:T(8,128)}, f32[4,128,128]{2,1,0:T(8,128)}, f32[32,128]{1,0:T(8,128)}) custom-call(s32[6]{0:T(128)} %owner_ids.1, s32[6,128]{1,0:T(8,128)} %obs_cell.1, f32[6,128]{1,0:T(8,128)} %observed.1, f32[6,128]{1,0:T(8,128)} %variance.1, f32[80,32,128]{2,1,0:T(8,128)} %bitcast.6, f32[6,32,128]{2,1,0:T(8,128)} %bitcast.9), custom_call_target="tpu_custom_call" | custom-call | flops 1000000000 | bytes 4000000 | tf_op jit(solution)/shard_map/pallas_call | solution.py:475
  67.7 5.2 %shard_map.78 = (f32[80,32,128]{2,1,0:T(8,128)}, f32[6,80,128]{2,1,0:T(8,128)}) custom-call(f32[80,4096]{1,0:T(8,128)} %get-tuple-element.8.slab, f32[6,80,128]{2,1,0:T(8,128)} %get-tuple-element.9.incs, f32[4,128,128]{2,1,0:T(8,128)} %get-tuple-element.10.factors, f32[32,128]{1,0:T(8,128)} %get-tuple-element.11.weights), custom_call_target="tpu_custom_call" | custom-call | tf_op jit(solution)/shard_map/pallas_call | solution.py:451
